TPU v7x, 128 devices: a whole 4x4x4 slice. The times are simulated.
128 devices in a mesh: fsdp: 8 (over z, x_hi), tp: 16 (over x_lo, y, core).
Axes of the slice: x: 4 (x_hi: 2, x_lo: 2; x = x_hi * 2 + x_lo), y: 4, z: 4, core: 2. Of those that a mesh axis runs over, the one named last changes fastest.
Arguments:
- momentum: float32 [3584, 18432], P('fsdp', 'tp'), may hold values from -1500 to 1500
Outputs:
- update: float32 [3584, 18432], P('fsdp', 'tp')
All inputs are finite; a program needn't handle non-finite values.
Results may differ from a plain program's by a relative error of at most 0.008.
Values may be sent and summed in bfloat16 or wider, within the bound.
No kernel may reach another device: no remote copies, remote signals or barrier semaphores. Data moves between devices by JAX's collectives and lax.ppermute only.
A program may use at most 64 MiB of HBM per device.

v0:
```python
import functools
import math

import jax
import jax.numpy as jnp
import numpy as np
from jax import lax
from jax.experimental import pallas as pl
from jax.experimental.pallas import tpu as pltpu
from jax.sharding import Mesh, PartitionSpec as P

coef_linear = 3.4445
coef_cubic = -4.775
coef_quintic = 2.0315

NAMES = ("z", "xh", "xl", "y", "c")
SIZES = (4, 2, 2, 4, 2)
PLANE = ("xh", "xl", "y")
BF = jnp.bfloat16
F32 = jnp.float32
ROWS = 448
SUB = 224
TAIL = 240
COLS = 1152
ALL = 3584
TILE = 128
WIDE = 512
VMEM = 20 * 1024 * 1024
MOST = 57 * 1024 * 1024
HALF = 256
REST = ROWS - HALF

def flat(pos):
    index = 0
    for value, size in zip(pos, SIZES):
        index = index * size + value
    return index


def move(value, target):
    every = [(z, a, b, y, c) for z in range(4) for a in range(2) for b in range(2) for y in range(4) for c in range(2)]
    return lax.ppermute(value, NAMES, [(flat(pos), flat(target(*pos))) for pos in every])


def swap_z(value, by):
    return move(value, lambda z, xh, xl, y, c: (z ^ by, xh, xl, y, c))


def along_x(value, step):
    def target(z, xh, xl, y, c):
        x = (xh * 2 + xl - step) % 4
        return (z, x // 2, x % 2, y, c)

    return move(value, target)


def along_y(value, step):
    return move(value, lambda z, xh, xl, y, c: (z, xh, xl, (y - step) % 4, c))


def swap_x(value, by):
    return move(value, lambda z, xh, xl, y, c: (z, xh ^ (by >> 1), xl ^ (by & 1), y, c))


def swap_y(value, by):
    return move(value, lambda z, xh, xl, y, c: (z, xh, xl, y ^ by, c))


def other_core(value):
    return move(value, lambda z, xh, xl, y, c: (z, xh, xl, y, 1 - c))


def trade_roles(value):
    return move(value, lambda z, xh, xl, y, c: (z, c, xl, y, xh))


def struct(*shape, dtype=BF):
    return jax.ShapeDtypeStruct(shape, dtype)


def call(kernel, shapes, counts, name, flops, scratch=(), scalars_out=0, limit=VMEM):
    smem, vmem = counts
    n = len(shapes)
    return pl.pallas_call(
        kernel,
        out_shape=shapes,
        in_specs=[pl.BlockSpec(memory_space=pltpu.SMEM)] * smem + [pl.BlockSpec(memory_space=pltpu.VMEM)] * vmem,
        out_specs=[pl.BlockSpec(memory_space=pltpu.VMEM)] * (n - scalars_out)
        + [pl.BlockSpec(memory_space=pltpu.SMEM)] * scalars_out,
        scratch_shapes=list(scratch),
        compiler_params=pltpu.CompilerParams(vmem_limit_bytes=limit),
        cost_estimate=pl.CostEstimate(flops=flops, bytes_accessed=6 << 20, transcendentals=0),
        name=name,
    )


def split_value(value):
    lane = lax.broadcasted_iota(jnp.int32, (16, TILE), 1)
    whole = jnp.full((16, TILE), value, F32)
    high = whole.astype(BF).astype(F32)
    middle = (whole - high).astype(BF).astype(F32)
    low = whole - high - middle
    out = jnp.where(lane == 0, high, jnp.where(lane == 1, middle, jnp.where(lane == 2, low, 0.0)))
    return out.astype(BF)


def cast_kernel(in_ref, upper_ref, lower_ref):
    squares = jnp.zeros((8, COLS), F32)
    for i in range(0, ROWS, 32):
        block = in_ref[i : i + 32, :]
        if i < SUB:
            upper_ref[i : i + 32, :] = block.astype(BF)
        else:
            lower_ref[i - SUB : i - SUB + 32, :] = block.astype(BF)
        square = block * block
        squares += (square[:8] + square[8:16]) + (square[16:24] + square[24:])
    lower_ref[SUB:, :] = jnp.zeros((TAIL - SUB, COLS), BF)
    lower_ref[SUB:, :TILE] = split_value(jnp.sum(squares))


def cast(momentum):
    return call(cast_kernel, [struct(SUB, COLS), struct(TAIL, COLS)], (0, 1), "cast", 0)(momentum)


def pieces(refs):
    for ref in refs:
        step = ref.shape[0] // 2
        for i in range(2):
            yield ref[i * step : i * step + SUB, :]


def sum_of_squares(refs):
    total = jnp.zeros((16, TILE), F32)
    for ref in refs:
        if ref.shape[0] == 2 * TAIL:
            for i in range(2):
                total += ref[i * TAIL + SUB : (i + 1) * TAIL, :TILE].astype(F32)
    return jnp.sum(total) * 0.0625


def turn(upper_ref, lower_ref, turned):
    turned[:, :SUB] = upper_ref[:SUB, :].T
    turned[:, SUB:] = lower_ref[:SUB, :].T


def first_gram_kernel(upper_ref, lower_ref, out_ref, turned):
    turn(upper_ref, lower_ref, turned)
    gram_kernel(turned, upper_ref, lower_ref, out_ref)


def gram_kernel(turned_ref, *refs):
    for i, piece in enumerate(pieces(refs[:-1])):
        refs[-1][i] = jnp.dot(piece, turned_ref[...], preferred_element_type=F32).astype(BF)


def first_gram(upper, lower):
    flops = 2 * 4 * SUB * ROWS * COLS
    shapes = [struct(4, SUB, ROWS), struct(COLS, ROWS)]
    return call(first_gram_kernel, shapes, (0, 2), "gram", flops)(upper, lower)


def gram(turned, *parts):
    flops = 2 * 4 * SUB * ROWS * COLS
    return call(gram_kernel, [struct(4, SUB, ROWS)], (0, 1 + len(parts)), "gram", flops)(turned, *parts)[0]


def gram_more_kernel(count, index_ref, turned, done_ref, more_ref, *refs):
    parts, fresh, outs = refs[:count], refs[count : 2 * count], refs[2 * count : 2 * count + 8]
    value_ref, full = refs[2 * count + 8], refs[2 * count + 9 :]

    def store(n, block):
        for q in range(4):
            end = min(TILE, ROWS - q * TILE)
            full[q][index_ref[q * 16 + n], :, :end] = block[:, q * TILE : q * TILE + end]

    for n in range(4):
        store(n, done_ref[n])
        store(4 + n, more_ref[n])
    for n, piece in enumerate(pieces(fresh)):
        store(2 * count + n, jnp.dot(piece, turned[...], preferred_element_type=F32).astype(BF))
    for q in range(4):
        end = min(TILE, ROWS - q * TILE)
        for half in range(2):
            outs[2 * q + half][:, :, :end] = full[q][half * 8 : half * 8 + 8, :, :end]
            if end < TILE:
                outs[2 * q + half][:, :, end:] = jnp.zeros((8, SUB, TILE - end), BF)
    value_ref[0] = sum_of_squares(refs[: 2 * count])


def gram_more(index, turned, done, more, parts, fresh):
    count = len(parts)
    return call(
        functools.partial(gram_more_kernel, count),
        [struct(8, SUB, TILE)] * 8 + [struct(1, dtype=F32)],
        (1, 3 + 2 * count),
        "gram",
        2 * 2 * count * SUB * ROWS * COLS,
        [pltpu.VMEM((16, SUB, TILE), BF)] * 4,
        scalars_out=1,
    )(index, turned, done, more, *parts, *fresh)


def panel_kernel(order_ref, *refs):
    parts, out_ref = refs[:-1], refs[-1]
    for i, piece in enumerate(pieces(parts)):
        out_ref[order_ref[i]] = piece


def halve_kernel(*refs):
    keep, got, outs = refs[:4], refs[4:8], refs[8:]
    for q in range(4):
        for i in range(8):
            total = keep[q][i].astype(F32) + got[q][i].astype(F32)
            outs[2 * q + i // 4][i % 4] = total.astype(BF)


def unstack_kernel(*refs):
    keep, got, outs = refs[:4], refs[4:8], refs[8:]
    for q in range(4):
        at = (q % 2) * TILE
        for i in range(4):
            total = keep[q][i].astype(F32) + got[q][i].astype(F32)
            outs[(q // 2) * 4 + i][:, at : at + TILE] = total.astype(BF)


def sum_kernel(value_ref, *refs):
    wides, rests, (out_ref, wide_ref, rest_ref) = refs[:4], refs[4:8], refs[8:]
    for refs, sum_ref in ((wides, wide_ref), (rests, rest_ref)):
        total = refs[0][...].astype(F32)
        for ref in refs[1:]:
            total += ref[...].astype(F32)
        sum_ref[...] = total.astype(BF)
    rest_ref[:16, REST:] = split_value(value_ref[0])[:, : HALF - REST]
    out_ref[:, :HALF] = wide_ref[...]
    out_ref[:, HALF:] = rest_ref[...]


def scatter_plane(split, value):
    keep, send = split[0::2], split[1::2]
    got = [swap_y(send[0], 3), swap_y(send[1], 1), swap_x(send[2], 3), swap_x(send[3], 1)]
    split = call(halve_kernel, [struct(4, SUB, TILE)] * 8, (0, 8), "halve", 0)(*keep, *got)
    keep, send = split[0::2], split[1::2]
    got = [swap_y(send[0], 1), swap_y(send[1], 3), swap_x(send[2], 1), swap_x(send[3], 3)]
    halves = call(unstack_kernel, [struct(SUB, HALF)] * 8, (0, 8), "unstack", 0)(*keep, *got)
    wides = [halves[0]] + [along_x(halves[s], -s) for s in (1, 2, 3)]
    rests = [halves[4]] + [along_y(halves[4 + s], -s) for s in (1, 2, 3)]
    shapes = [struct(SUB, WIDE), struct(SUB, HALF), struct(SUB, HALF)]
    return call(sum_kernel, shapes, (1, 8), "sum", 0)(value, *wides, *rests)


def stack_kernel(*refs):
    for n, outs in ((0, refs[8:10]), (4, refs[10:12])):
        for i in range(4):
            outs[0][i] = refs[n + i][:, :TILE]
            outs[1][i] = refs[n + i][:, TILE:]


def join_kernel(*refs):
    mine, got, outs = refs[:4], refs[4:8], refs[8:]
    for q in range(4):
        outs[q][:4] = mine[q][...]
        outs[q][4:] = got[q][...]


def gather_parts(wide, rest):
    wides = [wide] + [along_x(wide, s) for s in (1, 2, 3)]
    rests = [rest] + [along_y(rest, s) for s in (1, 2, 3)]
    parts = call(stack_kernel, [struct(4, SUB, TILE)] * 4, (0, 8), "stack", 0)(*wides, *rests)
    got = [swap_y(parts[0], 1), swap_y(parts[1], 3), swap_x(parts[2], 1), swap_x(parts[3], 3)]
    parts = call(join_kernel, [struct(8, SUB, TILE)] * 4, (0, 8), "join", 0)(*parts, *got)
    got = [swap_y(parts[0], 3), swap_y(parts[1], 1), swap_x(parts[2], 3), swap_x(parts[3], 1)]
    return [*parts, *got]


def place(pos_ref, refs, right, first=0):
    x, y = pos_ref[0], pos_ref[1]
    for q in range(first, first + len(refs) // 2):
        at = (q - first) * TILE
        end = min(TILE, right.shape[1] - at)
        near, far = ((1, 3), (3, 1))[q % 2]
        for i in range(16):
            by = (0, near, far, near ^ far)[i // 4]
            if q < 2:
                share = lax.rem(x + i % 4, 4) * 4 + (y ^ by)
            else:
                share = (x ^ by) * 4 + lax.rem(y + i % 4, 4)
            rows = pl.ds(pl.multiple_of(share * SUB, SUB), SUB)
            right[rows, at : at + end] = refs[q - first + (i // 8) * (len(refs) // 2)][i % 8, :, :end]


def product(core_ref, mine_ref, other_ref, right, left):
    first = core_ref[0] == 0
    for i in range(4):
        mine, other = mine_ref[i, :, :ROWS], other_ref[i, :, :ROWS]
        left[:, i * 896 : i * 896 + ROWS] = jnp.where(first, mine, other)
        left[:, i * 896 + ROWS : (i + 1) * 896] = jnp.where(first, other, mine)
    return jnp.dot(left[...], right[:, :ROWS], preferred_element_type=F32)


def first_kernel(core_ref, pos_ref, *refs):
    lefts, (share_ref, right_ref, out_ref, weight_ref, left) = refs[:4], refs[4:]
    squares = jnp.zeros((16, WIDE - ROWS), F32)
    for i in range(16):
        squares += right_ref[i * SUB : i * SUB + 16, ROWS:].astype(F32)
    squares = jnp.sum(squares) * 0.0625
    scale = 1.0 / (jnp.sqrt(jnp.full((8, TILE), squares, F32)) + 1e-07)
    scale = jnp.max(scale)
    twice = scale * scale
    first = core_ref[0] == 0
    for i, by in enumerate((0, 1, 3, 2)):
        rows = slice(i % 2 * SUB, (i % 2 + 1) * SUB)
        mine, other = lefts[i // 2][rows, :ROWS], lefts[2 + i // 2][rows, :ROWS]
        line = jnp.concatenate([jnp.where(first, mine, other), jnp.where(first, other, mine)], 1)
        left[:, pl.ds(pl.multiple_of((pos_ref[2] ^ by) * 896, TILE), 896)] = line
    total = jnp.dot(left[...], right_ref[:, :ROWS], preferred_element_type=F32)
    total = total * twice * (coef_quintic * twice) + (coef_cubic * twice) * share_ref[:, :ROWS].astype(F32)
    out_ref[...] = total.astype(BF)
    weight_ref[0] = twice
    weight_ref[1] = coef_linear * twice
    weight_ref[2] = scale * math.sqrt(18432)


def place_kernel(pos_ref, *refs):
    place(pos_ref, refs[:8], refs[8])


def first_mul(core, pos, lefts, share, right):
    return call(
        first_kernel,
        [struct(SUB, ROWS), struct(3, dtype=F32)],
        (2, 6),
        "first_mul",
        2 * SUB * ROWS * ALL,
        [pltpu.VMEM((SUB, ALL), BF)],
        scalars_out=1,
    )(core, pos, *lefts, share, right)


def mul_kernel(weights, count, core_ref, weight_ref, mine_ref, other_ref, right_ref, *refs):
    extras, outs, left = refs[:count], refs[count:-1], refs[-1]
    if weights is None:
        weights = [weight_ref[0], weight_ref[1]]
    total = product(core_ref, mine_ref, other_ref, right_ref, left) * weights[0]
    for weight, extra in zip(weights[1:], extras):
        total += weight * extra[:, :ROWS].astype(F32)
    total = total.astype(BF)
    if len(outs) == 1:
        outs[0][...] = total
    else:
        outs[0][...] = total[:, :HALF]
        outs[1][:, :REST] = total[:, HALF:]
        outs[1][:, REST:] = jnp.zeros((SUB, HALF - REST), BF)


def mul(core, weight, lefts, right, weights, extras, halves=False, limit=VMEM):
    return call(
        functools.partial(mul_kernel, weights, len(extras)),
        [struct(SUB, HALF)] * 2 if halves else [struct(SUB, ROWS)],
        (2, 3 + len(extras)),
        "mul",
        2 * SUB * ROWS * ALL,
        [pltpu.VMEM((SUB, ALL), BF)],
        limit=limit,
    )(core, weight, *lefts, right, *extras)


def own_rows(upper_ref, lower_ref, first, end):
    for base, ref in ((0, upper_ref), (SUB, lower_ref)):
        low, high = max(first, base), min(end, base + SUB)
        if low < high:
            yield low - first, ref[low - base : high - base, :]


def apply_kernel(first, weight_ref, pos_ref, upper_ref, lower_ref, panel_ref, *refs):
    parts, (out_ref, right, mat) = refs[:4], refs[4:]
    rows = out_ref.shape[0]
    place(pos_ref, parts, right, first // TILE)
    for k in range(4):
        mat[:, k * 896 : (k + 1) * 896] = right[k * 896 : (k + 1) * 896, :].T
    total = jnp.dot(mat[...], panel_ref[...], preferred_element_type=F32)
    linear = coef_linear * coef_linear
    for at, own in own_rows(upper_ref, lower_ref, first, first + rows):
        some = slice(at, at + own.shape[0])
        result = (total[some, :] + linear * own.astype(F32)) * weight_ref[2]
        out_ref[some, :] = result.astype(BF)


def apply(first, rows, weight, pos, upper, lower, panel, parts):
    return call(
        functools.partial(apply_kernel, first),
        [struct(rows, COLS)],
        (2, 7),
        "apply",
        2 * ALL * rows * COLS,
        [pltpu.VMEM((ALL, rows), BF), pltpu.VMEM((rows, ALL), BF)],
    )(weight, pos, upper, lower, panel, *parts)[0]


def gather_rows(value):
    mine = lax.all_gather(value, "z")
    return [mine, other_core(mine)]


def gather_plane(value):
    return lax.all_gather(value, PLANE, axis=0, tiled=True)


def body(momentum):
    z, c = (lax.axis_index(name).astype(jnp.int32) for name in ("z", "c"))
    core = c.reshape(1)
    x = (lax.axis_index("xh") * 2 + lax.axis_index("xl")).astype(jnp.int32)
    y = lax.axis_index("y").astype(jnp.int32)
    pos = jnp.stack([x, y, z])

    upper, lower = (trade_roles(value) for value in cast(momentum))
    upper_1 = swap_z(upper, 1)
    lower_3 = swap_z(lower, 3)
    uppers = jnp.concatenate([upper, upper_1], 0)
    lowers = jnp.concatenate([lower, lower_3], 0)
    uppers_3 = swap_z(uppers, 3)
    lowers_1 = swap_z(lowers, 1)
    done, turned = first_gram(uppers, lowers)
    near_0, near_1, uppers_3, lowers_1, done = lax.optimization_barrier((uppers, lowers, uppers_3, lowers_1, done))
    early = [uppers, lowers, uppers_3, lowers_1]
    late = [other_core(part) for part in (uppers_3, lowers_1, near_0, near_1)]
    more = gram(turned, uppers_3, lowers_1)
    near_at, far_at = ((0, 0), (1, 0), (0, 1), (3, 1)), ((3, 0), (2, 0), (1, 1), (2, 1))
    places = [(by, 0, half) for by, half in near_at + far_at] + [(by, 1, half) for by, half in far_at + near_at]
    by, swap, half = (np.array(column, np.int32) for column in zip(*places))
    piece_x = z ^ by
    piece_y = (c ^ swap) * 2 + half
    order = piece_x * 4 + piece_y

    gray_x, gray_y = ((e ^ (e >> 1)) * 4 for e in (piece_x ^ x, piece_y ^ y))
    flip_x, flip_y = (((g & 4) * 2 + (g >> 1 & 4)) for g in (gray_x, gray_y))
    far_x, far_y = (piece_x - x) & 3, (piece_y - y) & 3
    index = jnp.concatenate([gray_y + far_x, flip_y + far_x, gray_x + far_y, flip_x + far_y])
    *split, value = gram_more(index, turned, done, more, early, late)
    a, wide, rest = scatter_plane(split, value)
    near = jnp.concatenate([a, swap_z(a, 1)], 0)
    far = swap_z(near, 3)
    lefts = [near, far, other_core(near), other_core(far)]
    a_right = call(place_kernel, [struct(ALL, WIDE)], (1, 8), "place", 0)(pos, *gather_parts(wide, rest))[0]
    b, weight = first_mul(core, pos, lefts, a, a_right)

    b_right = gather_plane(b)
    (v,) = mul(core, weight, gather_rows(b), a_right, None, (a,))
    (a2,) = mul(core, weight, gather_rows(v), b_right, (1.0, coef_linear), (v,), limit=MOST)

    a2_right = gather_plane(a2)
    (h,) = mul(core, weight, gather_rows(a2), b_right, (1.0, coef_linear), (a2,))
    weights = (coef_quintic, coef_cubic, coef_linear)
    wide, rest = mul(core, weight, gather_rows(h), a2_right, weights, (h, b), halves=True, limit=MOST)
    wide, rest, order = lax.optimization_barrier((wide, rest, order))
    panel = call(panel_kernel, [struct(16, SUB, COLS)], (1, 8), "panel", 0)(order, *early, *late)[0]
    panel = panel.reshape(ALL, COLS)

    parts = gather_parts(wide, rest)
    head = trade_roles(apply(0, HALF, weight, pos, upper, lower, panel, parts[:2] + parts[4:6]))
    tail = trade_roles(apply(HALF, REST, weight, pos, upper, lower, panel, parts[2:4] + parts[6:]))
    return jnp.concatenate([head, tail], 0).astype(F32)


def solution(mesh):
    split = Mesh(mesh.devices.reshape(SIZES), NAMES)
    placed = P(("z", "xh"), ("xl", "y", "c"))
    return jax.shard_map(body, mesh=split, in_specs=(placed,), out_specs=placed, check_vma=False)
```

profile of v0, /device:TPU:1, one launch (start us, length us, event | category | flops | bytes accessed | tf_op | source)
XLA Modules:
  0.0 332.9 jit_solution(7090418377754960453)
XLA Ops:
  8.4 6.0 %collective-permute-start.2 = (bf16[240,1152]{1,0:T(8,128)(2,1)S(1)}, bf16[240,1152]{1,0:T(8,128)(2,1)S(1)}, u32[]{:S(2)}, u32[]{:S(2)}) collective-permute-start(bf16[240,1152]{1,0:T(8,128)(2,1)S(1)} %get-tuple-element.66), channel_id=1, source_target_pairs={{0,0},{1,16},{2,2},{3,18},{4,4},{5,20},{6,6},{7,22},{8,8},{9,24},{... | collective-permute-start | bytes 1658888 | tf_op jit(solution)/shard_map/ppermute | solution.py:42
  16.4 5.2 %collective-permute-done.2.lower_ref = bf16[240,1152]{1,0:T(8,128)(2,1)S(1)} collective-permute-done((bf16[240,1152]{1,0:T(8,128)(2,1)S(1)}, bf16[240,1152]{1,0:T(8,128)(2,1)S(1)}, u32[]{:S(2)}, u32[]{:S(2)}) %collective-permute-start.2) | collective-permute-done | bytes 552992 | tf_op jit(solution)/shard_map/ppermute | solution.py:42
  21.7 3.8 %collective-permute-start.3 = (bf16[240,1152]{1,0:T(8,128)(2,1)S(1)}, bf16[240,1152]{1,0:T(8,128)(2,1)S(1)}, u32[]{:S(2)}, u32[]{:S(2)}) collective-permute-start(bf16[240,1152]{1,0:T(8,128)(2,1)S(1)} %collective-permute-done.2.lower_ref), channel_id=1, source_target_pairs={{0,96},{1,97},{2,98},{3,99},{4,100},{5,101},{6,102},{7,103},{8,104... | collective-permute-start | bytes 1658888 | tf_op jit(solution)/shard_map/ppermute | solution.py:42
  29.7 5.8 %collective-permute-done.3 = bf16[240,1152]{1,0:T(8,128)(2,1)S(1)} collective-permute-done((bf16[240,1152]{1,0:T(8,128)(2,1)S(1)}, bf16[240,1152]{1,0:T(8,128)(2,1)S(1)}, u32[]{:S(2)}, u32[]{:S(2)}) %collective-permute-start.3) | collective-permute-done | bytes 552992 | tf_op jit(solution)/shard_map/ppermute | solution.py:42
  35.7 5.5 %collective-permute-done.1 = bf16[224,1152]{1,0:T(8,128)(2,1)S(1)} collective-permute-done((bf16[224,1152]{1,0:T(8,128)(2,1)S(1)}, bf16[224,1152]{1,0:T(8,128)(2,1)S(1)}, u32[]{:S(2)}, u32[]{:S(2)}) %collective-permute-start.1) | collective-permute-done | bytes 516128 | tf_op jit(solution)/shard_map/ppermute | solution.py:42
  42.0 3.6 %collective-permute-start.4 = (bf16[448,1152]{1,0:T(8,128)(2,1)}, bf16[448,1152]{1,0:T(8,128)(2,1)S(1)}, u32[]{:S(2)}, u32[]{:S(2)}) collective-permute-start(bf16[448,1152]{1,0:T(8,128)(2,1)} %constant_dynamic-update-slice_fusion.upper_ref.refs_0_), channel_id=1, source_target_pairs={{0,96},{1,97},{2,98},{3,99},{4,100},{5,101},{6,102},{7,103},{8,104... | collective-permute-start | bytes 3096584 | tf_op jit(solution)/shard_map/ppermute | solution.py:42
  50.6 7.3 %collective-permute-done.4.refs_0_.refs_2_ = bf16[448,1152]{1,0:T(8,128)(2,1)S(1)} collective-permute-done((bf16[448,1152]{1,0:T(8,128)(2,1)}, bf16[448,1152]{1,0:T(8,128)(2,1)S(1)}, u32[]{:S(2)}, u32[]{:S(2)}) %collective-permute-start.4) | collective-permute-done | bytes 1032224 | tf_op jit(solution)/shard_map/ppermute | solution.py:42
  61.6 3.6 %collective-permute-done.6.refs_4_ = bf16[448,1152]{1,0:T(8,128)(2,1)} collective-permute-done((bf16[448,1152]{1,0:T(8,128)(2,1)S(1)}, bf16[448,1152]{1,0:T(8,128)(2,1)}, u32[]{:S(2)}, u32[]{:S(2)}) %collective-permute-start.6) | collective-permute-done | bytes 1032224 | tf_op jit(solution)/shard_map/ppermute | solution.py:42
  65.3 6.3 %gram.5 = (bf16[8,224,128]{2,1,0:T(8,128)(2,1)S(1)}, bf16[8,224,128]{2,1,0:T(8,128)(2,1)S(1)}, bf16[8,224,128]{2,1,0:T(8,128)(2,1)S(1)}, bf16[8,224,128]{2,1,0:T...) custom-call(s32[64]{0:T(128)S(1)} %pad_add_fusion.1.index_ref, ...), custom_call_target="tpu_custom_call" | custom-call | flops 1849688064 | bytes 6291456 | tf_op jit(solution)/shard_map/gram/pallas_call | solution.py:192
  77.9 7.1 %collective-permute-done.10.refs_4_ = bf16[8,224,128]{2,1,0:T(8,128)(2,1)S(1)} collective-permute-done((bf16[8,224,128]{2,1,0:T(8,128)(2,1)S(1)}, bf16[8,224,128]{2,1,0:T(8,128)(2,1)S(1)}, u32[]{:S(2)}, u32[]{:S(2)}) %collective-permute-start.10) | collective-permute-done | bytes 458784 | tf_op jit(solution)/shard_map/ppermute | solution.py:42
  101.2 3.6 %collective-permute-start.22 = (bf16[224,256]{1,0:T(8,128)(2,1)S(1)}, bf16[224,256]{1,0:T(8,128)(2,1)S(1)}, u32[]{:S(2)}, u32[]{:S(2)}) collective-permute-start(bf16[224,256]{1,0:T(8,128)(2,1)S(1)} %get-tuple-element.97), channel_id=1, source_target_pairs={{0,4},{1,5},{2,6},{3,7},{4,0},{5,1},{6,2},{7,3},{8,12},{9,13},{10,... | collective-permute-start | bytes 344072 | tf_op jit(solution)/shard_map/ppermute | solution.py:42
  133.5 14.2 %collective-permute-start.26 = (bf16[448,512]{1,0:T(8,128)(2,1)S(1)}, bf16[448,512]{1,0:T(8,128)(2,1)S(1)}, u32[]{:S(2)}, u32[]{:S(2)}) collective-permute-start(bf16[448,512]{1,0:T(8,128)(2,1)S(1)} %constant_dynamic-update-slice_fusion.4.refs_0_), channel_id=1, source_target_pairs={{0,1},{1,0},{2,3},{3,2},{4,5},{5,4},{6,7},{7,6},{8,9},{9,8},{10,11... | collective-permute-start | bytes 1376264 | tf_op jit(solution)/shard_map/ppermute | solution.py:42
  147.7 4.3 %collective-permute-start.27 = (bf16[448,512]{1,0:T(8,128)(2,1)S(1)}, bf16[448,512]{1,0:T(8,128)(2,1)S(1)}, u32[]{:S(2)}, u32[]{:S(2)}) collective-permute-start(bf16[448,512]{1,0:T(8,128)(2,1)S(1)} %collective-permute-done.25.refs_1_), channel_id=1, source_target_pairs={{0,1},{1,0},{2,3},{3,2},{4,5},{5,4},{6,7},{7,6},{8,9},{9,8},{10,11... | collective-permute-start | bytes 1376264 | tf_op jit(solution)/shard_map/ppermute | solution.py:42
  156.6 12.1 %all-gather = bf16[896,448]{1,0:T(8,128)(2,1)S(1)} all-gather(bf16[224,448]{1,0:T(8,128)(2,1)} %copy-done.12), channel_id=2, replica_groups=mesh['z'=4,'xh'=2,'xl'=2,'y'=4,'c'=2] {'z'}, dimensions={0}, use_global_device_ids=true | all-gather | bytes 1003520 | tf_op jit(solution)/shard_map/all_gather | solution.py:400
  168.7 6.9 %collective-permute-start.42 = (bf16[4,224,448]{2,1,0:T(8,128)(2,1)S(1)}, bf16[4,224,448]{2,1,0:T(8,128)(2,1)S(1)}, u32[]{:S(2)}, u32[]{:S(2)}) collective-permute-start(bf16[4,224,448]{2,1,0:T(8,128)(2,1)S(1)} %bitcast.11), channel_id=1, source_target_pairs={{0,1},{1,0},{2,3},{3,2},{4,5},{5,4},{6,7},{7,6},{8,9},{9,8},{10,11... | collective-permute-start | bytes 2408456 | tf_op jit(solution)/shard_map/ppermute | solution.py:42
  182.1 12.3 %all-gather.1 = bf16[896,448]{1,0:T(8,128)(2,1)S(1)} all-gather(bf16[224,448]{1,0:T(8,128)(2,1)S(1)} %mul.58.refs_0_), channel_id=3, replica_groups=mesh['z'=4,'xh'=2,'xl'=2,'y'=4,'c'=2] {'z'}, dimensions={0}, use_global_device_ids=true | all-gather | bytes 1003520 | tf_op jit(solution)/shard_map/all_gather | solution.py:400
  199.8 7.9 %all-gather.7.cloned.1.call-done.right_ref = bf16[3584,448]{1,0:T(8,128)(2,1)} async-done(((bf16[224,448]{1,0:T(8,128)(2,1)}), bf16[3584,448]{1,0:T(8,128)(2,1)}) %all-gather.7.cloned.1.call-update) | async-done | bytes 3211280 | tf_op jit(solution)/shard_map/all_gather | solution.py:405
  207.7 4.3 %mul.59.refs_0_ = bf16[224,448]{1,0:T(8,128)(2,1)} custom-call(s32[1]{0:T(128)} %bitcast.core_ref, f32[3]{0:T(128)} %copy-done.19, bf16[4,224,448]{2,1,0:T(8,128)(2,1)} %bitcast.18, bf16[4,224,448]{2,1,0:T(8,128)(2,1)} %collective-permute-done.43.other_ref, bf16[3584,448]{1,0:T(8,128)(2,1)} %all-gather.7.cloned.1.call-done.right_ref, bf16[224,448]{1,0:T(8,128)(2,1)} %copy-done.14), custom_call_target="tpu_custom_call" | custom-call | flops 719323136 | bytes 6291456 | tf_op jit(solution)/shard_map/mul/pallas_call | solution.py:356
  212.1 13.4 %all-gather.2 = bf16[896,448]{1,0:T(8,128)(2,1)S(1)} all-gather(bf16[224,448]{1,0:T(8,128)(2,1)} %mul.59.refs_0_), channel_id=4, replica_groups=mesh['z'=4,'xh'=2,'xl'=2,'y'=4,'c'=2] {'z'}, dimensions={0}, use_global_device_ids=true | all-gather | bytes 1003520 | tf_op jit(solution)/shard_map/all_gather | solution.py:400
  234.4 13.5 %all-gather.3 = bf16[896,448]{1,0:T(8,128)(2,1)S(1)} all-gather(bf16[224,448]{1,0:T(8,128)(2,1)S(1)} %mul.60.refs_0_), channel_id=5, replica_groups=mesh['z'=4,'xh'=2,'xl'=2,'y'=4,'c'=2] {'z'}, dimensions={0}, use_global_device_ids=true | all-gather | bytes 1003520 | tf_op jit(solution)/shard_map/all_gather | solution.py:400
  252.6 8.3 %all-gather.9.cloned.1.call-done.right_ref = bf16[3584,448]{1,0:T(8,128)(2,1)} async-done(((bf16[224,448]{1,0:T(8,128)(2,1)}), bf16[3584,448]{1,0:T(8,128)(2,1)}) %all-gather.9.cloned.1.call-update) | async-done | bytes 3211280 | tf_op jit(solution)/shard_map/all_gather | solution.py:405
  261.0 4.4 %mul.61 = (bf16[224,256]{1,0:T(8,128)(2,1)}, bf16[224,256]{1,0:T(8,128)(2,1)}) custom-call(s32[1]{0:T(128)} %bitcast.core_ref, f32[3]{0:T(128)} %copy-done.19, bf16[4,224,448]{2,1,0:T(8,128)(2,1)} %bitcast.16, bf16[4,224,448]{2,1,0:T(8,128)(2,1)} %collective-permute-done.45.other_ref, bf16[3584,448]{1,0:T(8,128)(2,1)} %all-gather.9.cloned.1.call-done.right_ref, ...), custom_call_target="tpu_custom_call" | custom-call | flops 719323136 | bytes 6291456 | tf_op jit(solution)/shard_map/mul/pallas_call | solution.py:356
  300.4 10.0 %collective-permute-start.58 = (bf16[256,1152]{1,0:T(8,128)(2,1)S(1)}, bf16[256,1152]{1,0:T(8,128)(2,1)S(1)}, u32[]{:S(2)}, u32[]{:S(2)}) collective-permute-start(bf16[256,1152]{1,0:T(8,128)(2,1)S(1)} %apply.2), channel_id=1, source_target_pairs={{0,0},{1,16},{2,2},{3,18},{4,4},{5,20},{6,6},{7,22},{8,8},{9,24},{... | collective-permute-start | bytes 1769480 | tf_op jit(solution)/shard_map/ppermute | solution.py:42
  315.4 9.2 %collective-permute-done.61 = bf16[192,1152]{1,0:T(8,128)(2,1)S(1)} collective-permute-done((bf16[192,1152]{1,0:T(8,128)(2,1)S(1)}, bf16[192,1152]{1,0:T(8,128)(2,1)S(1)}, u32[]{:S(2)}, u32[]{:S(2)}) %collective-permute-start.61) | collective-permute-done | bytes 442400 | tf_op jit(solution)/shard_map/ppermute | solution.py:42
  (194 shorter events, 140.4 us)
Async XLA Ops:
  6.5 201.2 %all-gather.7.cloned.1.call-start = ((), (), s32[]{:S(2)}) async-start(), calls=%async_computation | async-start | bytes 3899392 | tf_op jit(solution)/shard_map/all_gather | solution.py:405
  8.4 13.2 %collective-permute-start.2 = (bf16[240,1152]{1,0:T(8,128)(2,1)S(1)}, bf16[240,1152]{1,0:T(8,128)(2,1)S(1)}, u32[]{:S(2)}, u32[]{:S(2)}) collective-permute-start(bf16[240,1152]{1,0:T(8,128)(2,1)S(1)} %get-tuple-element.66), channel_id=1, source_target_pairs={{0,0},{1,16},{2,2},{3,18},{4,4},{5,20},{6,6},{7,22},{8,8},{9,24},{... | collective-permute-start | bytes 1658888 | tf_op jit(solution)/shard_map/ppermute | solution.py:42
  14.5 12.7 %collective-permute-start = (bf16[224,1152]{1,0:T(8,128)(2,1)S(1)}, bf16[224,1152]{1,0:T(8,128)(2,1)S(1)}, u32[]{:S(2)}, u32[]{:S(2)}) collective-permute-start(bf16[224,1152]{1,0:T(8,128)(2,1)S(1)} %get-tuple-element.65), channel_id=1, source_target_pairs={{0,0},{1,16},{2,2},{3,18},{4,4},{5,20},{6,6},{7,22},{8,8},{9,24},{... | collective-permute-start | bytes 1548296 | tf_op jit(solution)/shard_map/ppermute | solution.py:42
  21.7 13.8 %collective-permute-start.3 = (bf16[240,1152]{1,0:T(8,128)(2,1)S(1)}, bf16[240,1152]{1,0:T(8,128)(2,1)S(1)}, u32[]{:S(2)}, u32[]{:S(2)}) collective-permute-start(bf16[240,1152]{1,0:T(8,128)(2,1)S(1)} %collective-permute-done.2.lower_ref), channel_id=1, source_target_pairs={{0,96},{1,97},{2,98},{3,99},{4,100},{5,101},{6,102},{7,103},{8,104... | collective-permute-start | bytes 1658888 | tf_op jit(solution)/shard_map/ppermute | solution.py:42
  27.2 14.0 %collective-permute-start.1 = (bf16[224,1152]{1,0:T(8,128)(2,1)S(1)}, bf16[224,1152]{1,0:T(8,128)(2,1)S(1)}, u32[]{:S(2)}, u32[]{:S(2)}) collective-permute-start(bf16[224,1152]{1,0:T(8,128)(2,1)S(1)} %collective-permute-done.upper_ref), channel_id=1, source_target_pairs={{0,32},{1,33},{2,34},{3,35},{4,36},{5,37},{6,38},{7,39},{8,40},{9,... | collective-permute-start | bytes 1548296 | tf_op jit(solution)/shard_map/ppermute | solution.py:42
  35.6 22.3 %collective-permute-start.5 = (bf16[480,1152]{1,0:T(8,128)(2,1)S(1)}, bf16[480,1152]{1,0:T(8,128)(2,1)S(1)}, u32[]{:S(2)}, u32[]{:S(2)}) collective-permute-start(bf16[480,1152]{1,0:T(8,128)(2,1)S(1)} %constant_dynamic-update-slice_fusion.2.lower_ref.refs_1_), channel_id=1, source_target_pairs={{0,32},{1,33},{2,34},{3,35},{4,36},{5,37},{6,38},{7,39},{8,40},{9,... | collective-permute-start | bytes 3317768 | tf_op jit(solution)/shard_map/ppermute | solution.py:42
  42.0 15.8 %collective-permute-start.4 = (bf16[448,1152]{1,0:T(8,128)(2,1)}, bf16[448,1152]{1,0:T(8,128)(2,1)S(1)}, u32[]{:S(2)}, u32[]{:S(2)}) collective-permute-start(bf16[448,1152]{1,0:T(8,128)(2,1)} %constant_dynamic-update-slice_fusion.upper_ref.refs_0_), channel_id=1, source_target_pairs={{0,96},{1,97},{2,98},{3,99},{4,100},{5,101},{6,102},{7,103},{8,104... | collective-permute-start | bytes 3096584 | tf_op jit(solution)/shard_map/ppermute | solution.py:42
  71.6 13.4 %collective-permute-start.10 = (bf16[8,224,128]{2,1,0:T(8,128)(2,1)S(1)}, bf16[8,224,128]{2,1,0:T(8,128)(2,1)S(1)}, u32[]{:S(2)}, u32[]{:S(2)}) collective-permute-start(bf16[8,224,128]{2,1,0:T(8,128)(2,1)S(1)} %get-tuple-element.79), channel_id=1, source_target_pairs={{0,6},{1,7},{2,4},{3,5},{4,2},{5,3},{6,0},{7,1},{8,14},{9,15},{10,... | collective-permute-start | bytes 1376264 | tf_op jit(solution)/shard_map/ppermute | solution.py:42
  74.4 11.7 %collective-permute-start.11 = (bf16[8,224,128]{2,1,0:T(8,128)(2,1)S(1)}, bf16[8,224,128]{2,1,0:T(8,128)(2,1)S(1)}, u32[]{:S(2)}, u32[]{:S(2)}) collective-permute-start(bf16[8,224,128]{2,1,0:T(8,128)(2,1)S(1)} %get-tuple-element.80), channel_id=1, source_target_pairs={{0,2},{1,3},{2,0},{3,1},{4,6},{5,7},{6,4},{7,5},{8,10},{9,11},{10,... | collective-permute-start | bytes 1376264 | tf_op jit(solution)/shard_map/ppermute | solution.py:42
  74.4 13.6 %collective-permute-start.12 = (bf16[8,224,128]{2,1,0:T(8,128)(2,1)S(1)}, bf16[8,224,128]{2,1,0:T(8,128)(2,1)S(1)}, u32[]{:S(2)}, u32[]{:S(2)}) collective-permute-start(bf16[8,224,128]{2,1,0:T(8,128)(2,1)S(1)} %get-tuple-element.81), channel_id=1, source_target_pairs={{0,24},{1,25},{2,26},{3,27},{4,28},{5,29},{6,30},{7,31},{8,16},{9,... | collective-permute-start | bytes 1376264 | tf_op jit(solution)/shard_map/ppermute | solution.py:42
  77.9 10.9 %collective-permute-start.13 = (bf16[8,224,128]{2,1,0:T(8,128)(2,1)S(1)}, bf16[8,224,128]{2,1,0:T(8,128)(2,1)S(1)}, u32[]{:S(2)}, u32[]{:S(2)}) collective-permute-start(bf16[8,224,128]{2,1,0:T(8,128)(2,1)S(1)} %get-tuple-element.82), channel_id=1, source_target_pairs={{0,8},{1,9},{2,10},{3,11},{4,12},{5,13},{6,14},{7,15},{8,0},{9,1},... | collective-permute-start | bytes 1376264 | tf_op jit(solution)/shard_map/ppermute | solution.py:42
  114.9 10.0 %collective-permute-start.24 = (bf16[224,512]{1,0:T(8,128)(2,1)S(1)}, bf16[224,512]{1,0:T(8,128)(2,1)S(1)}, u32[]{:S(2)}, u32[]{:S(2)}) collective-permute-start(bf16[224,512]{1,0:T(8,128)(2,1)S(1)} %get-tuple-element.99.refs_4_.refs_0_), channel_id=1, source_target_pairs={{0,32},{1,33},{2,34},{3,35},{4,36},{5,37},{6,38},{7,39},{8,40},{9,... | collective-permute-start | bytes 688136 | tf_op jit(solution)/shard_map/ppermute | solution.py:42
  120.5 8.7 %collective-permute-start.35 = (bf16[4,224,128]{2,1,0:T(8,128)(2,1)S(1)}, bf16[4,224,128]{2,1,0:T(8,128)(2,1)S(1)}, u32[]{:S(2)}, u32[]{:S(2)}) collective-permute-start(bf16[4,224,128]{2,1,0:T(8,128)(2,1)S(1)} %get-tuple-element.103.refs_1_), channel_id=1, source_target_pairs={{0,6},{1,7},{2,4},{3,5},{4,2},{5,3},{6,0},{7,1},{8,14},{9,15},{10,... | collective-permute-start | bytes 688136 | tf_op jit(solution)/shard_map/ppermute | solution.py:42
  129.3 18.4 %collective-permute-start.38 = (bf16[8,224,128]{2,1,0:T(8,128)(2,1)S(1)}, bf16[8,224,128]{2,1,0:T(8,128)(2,1)S(1)}, u32[]{:S(2)}, u32[]{:S(2)}) collective-permute-start(bf16[8,224,128]{2,1,0:T(8,128)(2,1)S(1)} %get-tuple-element.106.refs_0_), channel_id=1, source_target_pairs={{0,6},{1,7},{2,4},{3,5},{4,2},{5,3},{6,0},{7,1},{8,14},{9,15},{10,... | collective-permute-start | bytes 1376264 | tf_op jit(solution)/shard_map/ppermute | solution.py:42
  130.3 21.8 %collective-permute-start.39 = (bf16[8,224,128]{2,1,0:T(8,128)(2,1)S(1)}, bf16[8,224,128]{2,1,0:T(8,128)(2,1)S(1)}, u32[]{:S(2)}, u32[]{:S(2)}) collective-permute-start(bf16[8,224,128]{2,1,0:T(8,128)(2,1)S(1)} %get-tuple-element.107.refs_1_), channel_id=1, source_target_pairs={{0,2},{1,3},{2,0},{3,1},{4,6},{5,7},{6,4},{7,5},{8,10},{9,11},{10,... | collective-permute-start | bytes 1376264 | tf_op jit(solution)/shard_map/ppermute | solution.py:42
  130.4 21.6 %collective-permute-start.40 = (bf16[8,224,128]{2,1,0:T(8,128)(2,1)S(1)}, bf16[8,224,128]{2,1,0:T(8,128)(2,1)S(1)}, u32[]{:S(2)}, u32[]{:S(2)}) collective-permute-start(bf16[8,224,128]{2,1,0:T(8,128)(2,1)S(1)} %get-tuple-element.108.refs_2_), channel_id=1, source_target_pairs={{0,24},{1,25},{2,26},{3,27},{4,28},{5,29},{6,30},{7,31},{8,16},{9,... | collective-permute-start | bytes 1376264 | tf_op jit(solution)/shard_map/ppermute | solution.py:42
  133.1 19.0 %collective-permute-start.41 = (bf16[8,224,128]{2,1,0:T(8,128)(2,1)S(1)}, bf16[8,224,128]{2,1,0:T(8,128)(2,1)S(1)}, u32[]{:S(2)}, u32[]{:S(2)}) collective-permute-start(bf16[8,224,128]{2,1,0:T(8,128)(2,1)S(1)} %get-tuple-element.109.refs_3_), channel_id=1, source_target_pairs={{0,8},{1,9},{2,10},{3,11},{4,12},{5,13},{6,14},{7,15},{8,0},{9,1},... | collective-permute-start | bytes 1376264 | tf_op jit(solution)/shard_map/ppermute | solution.py:42
  133.5 19.8 %collective-permute-start.26 = (bf16[448,512]{1,0:T(8,128)(2,1)S(1)}, bf16[448,512]{1,0:T(8,128)(2,1)S(1)}, u32[]{:S(2)}, u32[]{:S(2)}) collective-permute-start(bf16[448,512]{1,0:T(8,128)(2,1)S(1)} %constant_dynamic-update-slice_fusion.4.refs_0_), channel_id=1, source_target_pairs={{0,1},{1,0},{2,3},{3,2},{4,5},{5,4},{6,7},{7,6},{8,9},{9,8},{10,11... | collective-permute-start | bytes 1376264 | tf_op jit(solution)/shard_map/ppermute | solution.py:42
  156.5 104.5 %all-gather.9.cloned.1.call-start = ((), (), s32[]{:S(2)}) async-start(), calls=%async_computation.1 | async-start | bytes 3899392 | tf_op jit(solution)/shard_map/all_gather | solution.py:405
  168.7 9.0 %collective-permute-start.42 = (bf16[4,224,448]{2,1,0:T(8,128)(2,1)S(1)}, bf16[4,224,448]{2,1,0:T(8,128)(2,1)S(1)}, u32[]{:S(2)}, u32[]{:S(2)}) collective-permute-start(bf16[4,224,448]{2,1,0:T(8,128)(2,1)S(1)} %bitcast.11), channel_id=1, source_target_pairs={{0,1},{1,0},{2,3},{3,2},{4,5},{5,4},{6,7},{7,6},{8,9},{9,8},{10,11... | collective-permute-start | bytes 2408456 | tf_op jit(solution)/shard_map/ppermute | solution.py:42
  289.3 21.2 %collective-permute-start.59 = (bf16[8,224,128]{2,1,0:T(8,128)(2,1)S(1)}, bf16[8,224,128]{2,1,0:T(8,128)(2,1)S(1)}, u32[]{:S(2)}, u32[]{:S(2)}) collective-permute-start(bf16[8,224,128]{2,1,0:T(8,128)(2,1)S(1)} %get-tuple-element.123.refs_0_), channel_id=1, source_target_pairs={{0,24},{1,25},{2,26},{3,27},{4,28},{5,29},{6,30},{7,31},{8,16},{9,... | collective-permute-start | bytes 1376264 | tf_op jit(solution)/shard_map/ppermute | solution.py:42
  291.7 18.8 %collective-permute-start.60 = (bf16[8,224,128]{2,1,0:T(8,128)(2,1)S(1)}, bf16[8,224,128]{2,1,0:T(8,128)(2,1)S(1)}, u32[]{:S(2)}, u32[]{:S(2)}) collective-permute-start(bf16[8,224,128]{2,1,0:T(8,128)(2,1)S(1)} %get-tuple-element.124.refs_1_), channel_id=1, source_target_pairs={{0,8},{1,9},{2,10},{3,11},{4,12},{5,13},{6,14},{7,15},{8,0},{9,1},... | collective-permute-start | bytes 1376264 | tf_op jit(solution)/shard_map/ppermute | solution.py:42
  300.4 24.1 %collective-permute-start.58 = (bf16[256,1152]{1,0:T(8,128)(2,1)S(1)}, bf16[256,1152]{1,0:T(8,128)(2,1)S(1)}, u32[]{:S(2)}, u32[]{:S(2)}) collective-permute-start(bf16[256,1152]{1,0:T(8,128)(2,1)S(1)} %apply.2), channel_id=1, source_target_pairs={{0,0},{1,16},{2,2},{3,18},{4,4},{5,20},{6,6},{7,22},{8,8},{9,24},{... | collective-permute-start | bytes 1769480 | tf_op jit(solution)/shard_map/ppermute | solution.py:42
  313.5 11.1 %collective-permute-start.61 = (bf16[192,1152]{1,0:T(8,128)(2,1)S(1)}, bf16[192,1152]{1,0:T(8,128)(2,1)S(1)}, u32[]{:S(2)}, u32[]{:S(2)}) collective-permute-start(bf16[192,1152]{1,0:T(8,128)(2,1)S(1)} %apply.3), channel_id=1, source_target_pairs={{0,0},{1,16},{2,2},{3,18},{4,4},{5,20},{6,6},{7,22},{8,8},{9,24},{... | collective-permute-start | bytes 1327112 | tf_op jit(solution)/shard_map/ppermute | solution.py:42
  (67 other events, 481.2 us)
Sparse Core Ops, SparseCore 0:
  156.7 51.0 all-gather.6
  212.2 48.7 all-gather.8
where the time goes:
time: 333 us
  starting transfers between devices  109 us (33%)
  waiting for transfers between devices  102 us (31%)
  blocking collectives  51.3 us (15%)
  Pallas kernels  38.1 us (11%)
  local copies, waits for them, and re-layouts  16.8 us (5%)
  between operations  13.8 us (4%)
    ppermute x62, starting transfers between devices, move(): lax.ppermute(value, NAMES, [(flat(pos), flat(target(*pos))) for pos in ev...  109 us
    ppermute x62, waiting for transfers between devices, move(): lax.ppermute(value, NAMES, [(flat(pos), flat(target(*pos))) for pos in ev...  86 us
    all_gather x4, blocking collectives, gather_rows(): mine = lax.all_gather(value, 'z')  51.3 us
    all_gather x2, waiting for transfers between devices, gather_plane(): return lax.all_gather(value, PLANE, axis=0, tiled=True)  16.3 us
    unnamed x57, local copies, waits for them, and re-layouts  15.8 us
    pallas_call x4, Pallas kernels, mul(): call(functools.partial(mul_kernel, weights, len(extras)), [struct(SUB, HA...  11.8 us
  transfers between devices with their start and end apart: 64, of which 37 were waited for; matrix products, arithmetic and copies ran while one was open for 1% of the time, Pallas kernels for 6%

commit v1 on v0

--- a/solution.py
+++ b/solution.py
@@ -420,7 +420,7 @@
     uppers_3 = swap_z(uppers, 3)
     lowers_1 = swap_z(lowers, 1)
     done, turned = first_gram(uppers, lowers)
-    near_0, near_1, uppers_3, lowers_1, done = lax.optimization_barrier((uppers, lowers, uppers_3, lowers_1, done))
+    near_0, near_1, lowers_1, done = lax.optimization_barrier((uppers, lowers, lowers_1, done))
     early = [uppers, lowers, uppers_3, lowers_1]
     late = [other_core(part) for part in (uppers_3, lowers_1, near_0, near_1)]
     more = gram(turned, uppers_3, lowers_1)

time: 333 us -> 330 us (level)
  transfers between devices with their start and end apart: 64 -> 64, of which waited for: 37 -> 39; matrix products, arithmetic and copies ran while one was open for 1% -> 1% of each run, Pallas kernels for 6% -> 6%
where the time goes in v1:
time: 330 us
  starting transfers between devices  108 us (33%)
  waiting for transfers between devices  99.9 us (30%)
  blocking collectives  51.3 us (16%)
  Pallas kernels  38.1 us (12%)
  local copies, waits for them, and re-layouts  16.8 us (5%)
  between operations  13.8 us (4%)
    ppermute x62, starting transfers between devices, move(): lax.ppermute(value, NAMES, [(flat(pos), flat(target(*pos))) for pos in ev...  108 us
    ppermute x62, waiting for transfers between devices, move(): lax.ppermute(value, NAMES, [(flat(pos), flat(target(*pos))) for pos in ev...  83.6 us
    all_gather x4, blocking collectives, gather_rows(): mine = lax.all_gather(value, 'z')  51.3 us
    all_gather x2, waiting for transfers between devices, gather_plane(): return lax.all_gather(value, PLANE, axis=0, tiled=True)  16.3 us
    unnamed x57, local copies, waits for them, and re-layouts  15.8 us
    pallas_call x4, Pallas kernels, mul(): call(functools.partial(mul_kernel, weights, len(extras)), [struct(SUB, HA...  11.8 us
  transfers between devices with their start and end apart: 64, of which 39 were waited for; matrix products, arithmetic and copies ran while one was open for 1% of the time, Pallas kernels for 6%

profile of v1, /device:TPU:1, one launch (start us, length us, event | category | flops | bytes accessed | tf_op | source)
XLA Modules:
  0.0 329.9 jit_solution(8889463787405989499)
XLA Ops:
  8.4 6.0 %collective-permute-start.2 = (bf16[240,1152]{1,0:T(8,128)(2,1)S(1)}, bf16[240,1152]{1,0:T(8,128)(2,1)S(1)}, u32[]{:S(2)}, u32[]{:S(2)}) collective-permute-start(bf16[240,1152]{1,0:T(8,128)(2,1)S(1)} %get-tuple-element.65), channel_id=1, source_target_pairs={{0,0},{1,16},{2,2},{3,18},{4,4},{5,20},{6,6},{7,22},{8,8},{9,24},{... | collective-permute-start | bytes 1658888 | tf_op jit(solution)/shard_map/ppermute | solution.py:42
  16.4 5.2 %collective-permute-done.2.lower_ref = bf16[240,1152]{1,0:T(8,128)(2,1)S(1)} collective-permute-done((bf16[240,1152]{1,0:T(8,128)(2,1)S(1)}, bf16[240,1152]{1,0:T(8,128)(2,1)S(1)}, u32[]{:S(2)}, u32[]{:S(2)}) %collective-permute-start.2) | collective-permute-done | bytes 552992 | tf_op jit(solution)/shard_map/ppermute | solution.py:42
  21.7 3.8 %collective-permute-start.3 = (bf16[240,1152]{1,0:T(8,128)(2,1)S(1)}, bf16[240,1152]{1,0:T(8,128)(2,1)S(1)}, u32[]{:S(2)}, u32[]{:S(2)}) collective-permute-start(bf16[240,1152]{1,0:T(8,128)(2,1)S(1)} %collective-permute-done.2.lower_ref), channel_id=1, source_target_pairs={{0,96},{1,97},{2,98},{3,99},{4,100},{5,101},{6,102},{7,103},{8,104... | collective-permute-start | bytes 1658888 | tf_op jit(solution)/shard_map/ppermute | solution.py:42
  29.7 5.8 %collective-permute-done.3 = bf16[240,1152]{1,0:T(8,128)(2,1)S(1)} collective-permute-done((bf16[240,1152]{1,0:T(8,128)(2,1)S(1)}, bf16[240,1152]{1,0:T(8,128)(2,1)S(1)}, u32[]{:S(2)}, u32[]{:S(2)}) %collective-permute-start.3) | collective-permute-done | bytes 552992 | tf_op jit(solution)/shard_map/ppermute | solution.py:42
  35.7 5.5 %collective-permute-done.1 = bf16[224,1152]{1,0:T(8,128)(2,1)S(1)} collective-permute-done((bf16[224,1152]{1,0:T(8,128)(2,1)S(1)}, bf16[224,1152]{1,0:T(8,128)(2,1)S(1)}, u32[]{:S(2)}, u32[]{:S(2)}) %collective-permute-start.1) | collective-permute-done | bytes 516128 | tf_op jit(solution)/shard_map/ppermute | solution.py:42
  42.0 3.6 %collective-permute-start.5 = (bf16[448,1152]{1,0:T(8,128)(2,1)}, bf16[448,1152]{1,0:T(8,128)(2,1)S(1)}, u32[]{:S(2)}, u32[]{:S(2)}) collective-permute-start(bf16[448,1152]{1,0:T(8,128)(2,1)} %constant_dynamic-update-slice_fusion.upper_ref.refs_0_), channel_id=1, source_target_pairs={{0,96},{1,97},{2,98},{3,99},{4,100},{5,101},{6,102},{7,103},{8,104... | collective-permute-start | bytes 3096584 | tf_op jit(solution)/shard_map/ppermute | solution.py:42
  50.6 4.7 %collective-permute-done.4.refs_1_.refs_3_ = bf16[480,1152]{1,0:T(8,128)(2,1)S(1)} collective-permute-done((bf16[480,1152]{1,0:T(8,128)(2,1)S(1)}, bf16[480,1152]{1,0:T(8,128)(2,1)S(1)}, u32[]{:S(2)}, u32[]{:S(2)}) %collective-permute-start.4) | collective-permute-done | bytes 1105952 | tf_op jit(solution)/shard_map/ppermute | solution.py:42
  62.9 6.3 %gram.5 = (bf16[8,224,128]{2,1,0:T(8,128)(2,1)S(1)}, bf16[8,224,128]{2,1,0:T(8,128)(2,1)S(1)}, bf16[8,224,128]{2,1,0:T(8,128)(2,1)S(1)}, bf16[8,224,128]{2,1,0:T...) custom-call(s32[64]{0:T(128)S(1)} %pad_add_fusion.1.index_ref, ...), custom_call_target="tpu_custom_call" | custom-call | flops 1849688064 | bytes 6291456 | tf_op jit(solution)/shard_map/gram/pallas_call | solution.py:192
  75.0 7.6 %collective-permute-done.10.refs_4_ = bf16[8,224,128]{2,1,0:T(8,128)(2,1)S(1)} collective-permute-done((bf16[8,224,128]{2,1,0:T(8,128)(2,1)S(1)}, bf16[8,224,128]{2,1,0:T(8,128)(2,1)S(1)}, u32[]{:S(2)}, u32[]{:S(2)}) %collective-permute-start.10) | collective-permute-done | bytes 458784 | tf_op jit(solution)/shard_map/ppermute | solution.py:42
  98.2 3.6 %collective-permute-start.22 = (bf16[224,256]{1,0:T(8,128)(2,1)S(1)}, bf16[224,256]{1,0:T(8,128)(2,1)S(1)}, u32[]{:S(2)}, u32[]{:S(2)}) collective-permute-start(bf16[224,256]{1,0:T(8,128)(2,1)S(1)} %get-tuple-element.95), channel_id=1, source_target_pairs={{0,4},{1,5},{2,6},{3,7},{4,0},{5,1},{6,2},{7,3},{8,12},{9,13},{10,... | collective-permute-start | bytes 344072 | tf_op jit(solution)/shard_map/ppermute | solution.py:42
  130.6 14.2 %collective-permute-start.26 = (bf16[448,512]{1,0:T(8,128)(2,1)S(1)}, bf16[448,512]{1,0:T(8,128)(2,1)S(1)}, u32[]{:S(2)}, u32[]{:S(2)}) collective-permute-start(bf16[448,512]{1,0:T(8,128)(2,1)S(1)} %constant_dynamic-update-slice_fusion.4.refs_0_), channel_id=1, source_target_pairs={{0,1},{1,0},{2,3},{3,2},{4,5},{5,4},{6,7},{7,6},{8,9},{9,8},{10,11... | collective-permute-start | bytes 1376264 | tf_op jit(solution)/shard_map/ppermute | solution.py:42
  144.8 4.3 %collective-permute-start.27 = (bf16[448,512]{1,0:T(8,128)(2,1)S(1)}, bf16[448,512]{1,0:T(8,128)(2,1)S(1)}, u32[]{:S(2)}, u32[]{:S(2)}) collective-permute-start(bf16[448,512]{1,0:T(8,128)(2,1)S(1)} %collective-permute-done.25.refs_1_), channel_id=1, source_target_pairs={{0,1},{1,0},{2,3},{3,2},{4,5},{5,4},{6,7},{7,6},{8,9},{9,8},{10,11... | collective-permute-start | bytes 1376264 | tf_op jit(solution)/shard_map/ppermute | solution.py:42
  153.6 12.1 %all-gather = bf16[896,448]{1,0:T(8,128)(2,1)S(1)} all-gather(bf16[224,448]{1,0:T(8,128)(2,1)} %copy-done.12), channel_id=2, replica_groups=mesh['z'=4,'xh'=2,'xl'=2,'y'=4,'c'=2] {'z'}, dimensions={0}, use_global_device_ids=true | all-gather | bytes 1003520 | tf_op jit(solution)/shard_map/all_gather | solution.py:400
  165.7 6.9 %collective-permute-start.42 = (bf16[4,224,448]{2,1,0:T(8,128)(2,1)S(1)}, bf16[4,224,448]{2,1,0:T(8,128)(2,1)S(1)}, u32[]{:S(2)}, u32[]{:S(2)}) collective-permute-start(bf16[4,224,448]{2,1,0:T(8,128)(2,1)S(1)} %bitcast.11), channel_id=1, source_target_pairs={{0,1},{1,0},{2,3},{3,2},{4,5},{5,4},{6,7},{7,6},{8,9},{9,8},{10,11... | collective-permute-start | bytes 2408456 | tf_op jit(solution)/shard_map/ppermute | solution.py:42
  179.1 12.4 %all-gather.1 = bf16[896,448]{1,0:T(8,128)(2,1)S(1)} all-gather(bf16[224,448]{1,0:T(8,128)(2,1)S(1)} %mul.58.refs_0_), channel_id=3, replica_groups=mesh['z'=4,'xh'=2,'xl'=2,'y'=4,'c'=2] {'z'}, dimensions={0}, use_global_device_ids=true | all-gather | bytes 1003520 | tf_op jit(solution)/shard_map/all_gather | solution.py:400
  196.8 7.9 %all-gather.7.cloned.1.call-done.right_ref = bf16[3584,448]{1,0:T(8,128)(2,1)} async-done(((bf16[224,448]{1,0:T(8,128)(2,1)}), bf16[3584,448]{1,0:T(8,128)(2,1)}) %all-gather.7.cloned.1.call-update) | async-done | bytes 3211280 | tf_op jit(solution)/shard_map/all_gather | solution.py:405
  204.8 4.3 %mul.59.refs_0_ = bf16[224,448]{1,0:T(8,128)(2,1)} custom-call(s32[1]{0:T(128)} %bitcast.core_ref, f32[3]{0:T(128)} %copy-done.19, bf16[4,224,448]{2,1,0:T(8,128)(2,1)} %bitcast.18, bf16[4,224,448]{2,1,0:T(8,128)(2,1)} %collective-permute-done.43.other_ref, bf16[3584,448]{1,0:T(8,128)(2,1)} %all-gather.7.cloned.1.call-done.right_ref, bf16[224,448]{1,0:T(8,128)(2,1)} %copy-done.14), custom_call_target="tpu_custom_call" | custom-call | flops 719323136 | bytes 6291456 | tf_op jit(solution)/shard_map/mul/pallas_call | solution.py:356
  209.1 13.4 %all-gather.2 = bf16[896,448]{1,0:T(8,128)(2,1)S(1)} all-gather(bf16[224,448]{1,0:T(8,128)(2,1)} %mul.59.refs_0_), channel_id=4, replica_groups=mesh['z'=4,'xh'=2,'xl'=2,'y'=4,'c'=2] {'z'}, dimensions={0}, use_global_device_ids=true | all-gather | bytes 1003520 | tf_op jit(solution)/shard_map/all_gather | solution.py:400
  231.4 13.5 %all-gather.3 = bf16[896,448]{1,0:T(8,128)(2,1)S(1)} all-gather(bf16[224,448]{1,0:T(8,128)(2,1)S(1)} %mul.60.refs_0_), channel_id=5, replica_groups=mesh['z'=4,'xh'=2,'xl'=2,'y'=4,'c'=2] {'z'}, dimensions={0}, use_global_device_ids=true | all-gather | bytes 1003520 | tf_op jit(solution)/shard_map/all_gather | solution.py:400
  249.7 8.3 %all-gather.9.cloned.1.call-done.right_ref = bf16[3584,448]{1,0:T(8,128)(2,1)} async-done(((bf16[224,448]{1,0:T(8,128)(2,1)}), bf16[3584,448]{1,0:T(8,128)(2,1)}) %all-gather.9.cloned.1.call-update) | async-done | bytes 3211280 | tf_op jit(solution)/shard_map/all_gather | solution.py:405
  258.0 4.4 %mul.61 = (bf16[224,256]{1,0:T(8,128)(2,1)}, bf16[224,256]{1,0:T(8,128)(2,1)}) custom-call(s32[1]{0:T(128)} %bitcast.core_ref, f32[3]{0:T(128)} %copy-done.19, bf16[4,224,448]{2,1,0:T(8,128)(2,1)} %bitcast.16, bf16[4,224,448]{2,1,0:T(8,128)(2,1)} %collective-permute-done.45.other_ref, bf16[3584,448]{1,0:T(8,128)(2,1)} %all-gather.9.cloned.1.call-done.right_ref, ...), custom_call_target="tpu_custom_call" | custom-call | flops 719323136 | bytes 6291456 | tf_op jit(solution)/shard_map/mul/pallas_call | solution.py:356
  293.9 3.5 %apply.2 = bf16[256,1152]{1,0:T(8,128)(2,1)S(1)} custom-call(f32[3]{0:T(128)S(1)} %copy-done.21, s32[3]{0:T(128)S(1)} %pad_add_fusion.pos_ref, bf16[224,1152]{1,0:T(8,128)(2,1)S(1)} %copy-done.9, bf16[240,1152]{1,0:T(8,128)(2,1)S(1)} %copy-done.4, bf16[3584,1152]{1,0:T(8,128)(2,1)S(1)} %bitcast.9, bf16[8,224,128]{2,1,0:T(8,128)(2,1)S(1)} %get-tuple-element.119.refs_0_, ...), custom_call_target="tpu_custom_call" | custom-call | flops 2113929216 | bytes 6291456 | tf_op jit(solution)/shard_map/apply/pallas_call | solution.py:389
  297.5 10.0 %collective-permute-start.58 = (bf16[256,1152]{1,0:T(8,128)(2,1)S(1)}, bf16[256,1152]{1,0:T(8,128)(2,1)S(1)}, u32[]{:S(2)}, u32[]{:S(2)}) collective-permute-start(bf16[256,1152]{1,0:T(8,128)(2,1)S(1)} %apply.2), channel_id=1, source_target_pairs={{0,0},{1,16},{2,2},{3,18},{4,4},{5,20},{6,6},{7,22},{8,8},{9,24},{... | collective-permute-start | bytes 1769480 | tf_op jit(solution)/shard_map/ppermute | solution.py:42
  312.4 9.2 %collective-permute-done.61 = bf16[192,1152]{1,0:T(8,128)(2,1)S(1)} collective-permute-done((bf16[192,1152]{1,0:T(8,128)(2,1)S(1)}, bf16[192,1152]{1,0:T(8,128)(2,1)S(1)}, u32[]{:S(2)}, u32[]{:S(2)}) %collective-permute-start.61) | collective-permute-done | bytes 442400 | tf_op jit(solution)/shard_map/ppermute | solution.py:42
  (194 shorter events, 139.5 us)
Async XLA Ops:
  6.5 198.2 %all-gather.7.cloned.1.call-start = ((), (), s32[]{:S(2)}) async-start(), calls=%async_computation | async-start | bytes 3899392 | tf_op jit(solution)/shard_map/all_gather | solution.py:405
  8.4 13.2 %collective-permute-start.2 = (bf16[240,1152]{1,0:T(8,128)(2,1)S(1)}, bf16[240,1152]{1,0:T(8,128)(2,1)S(1)}, u32[]{:S(2)}, u32[]{:S(2)}) collective-permute-start(bf16[240,1152]{1,0:T(8,128)(2,1)S(1)} %get-tuple-element.65), channel_id=1, source_target_pairs={{0,0},{1,16},{2,2},{3,18},{4,4},{5,20},{6,6},{7,22},{8,8},{9,24},{... | collective-permute-start | bytes 1658888 | tf_op jit(solution)/shard_map/ppermute | solution.py:42
  14.5 12.7 %collective-permute-start = (bf16[224,1152]{1,0:T(8,128)(2,1)S(1)}, bf16[224,1152]{1,0:T(8,128)(2,1)S(1)}, u32[]{:S(2)}, u32[]{:S(2)}) collective-permute-start(bf16[224,1152]{1,0:T(8,128)(2,1)S(1)} %get-tuple-element.64), channel_id=1, source_target_pairs={{0,0},{1,16},{2,2},{3,18},{4,4},{5,20},{6,6},{7,22},{8,8},{9,24},{... | collective-permute-start | bytes 1548296 | tf_op jit(solution)/shard_map/ppermute | solution.py:42
  21.7 13.8 %collective-permute-start.3 = (bf16[240,1152]{1,0:T(8,128)(2,1)S(1)}, bf16[240,1152]{1,0:T(8,128)(2,1)S(1)}, u32[]{:S(2)}, u32[]{:S(2)}) collective-permute-start(bf16[240,1152]{1,0:T(8,128)(2,1)S(1)} %collective-permute-done.2.lower_ref), channel_id=1, source_target_pairs={{0,96},{1,97},{2,98},{3,99},{4,100},{5,101},{6,102},{7,103},{8,104... | collective-permute-start | bytes 1658888 | tf_op jit(solution)/shard_map/ppermute | solution.py:42
  27.2 14.0 %collective-permute-start.1 = (bf16[224,1152]{1,0:T(8,128)(2,1)S(1)}, bf16[224,1152]{1,0:T(8,128)(2,1)S(1)}, u32[]{:S(2)}, u32[]{:S(2)}) collective-permute-start(bf16[224,1152]{1,0:T(8,128)(2,1)S(1)} %collective-permute-done.upper_ref), channel_id=1, source_target_pairs={{0,32},{1,33},{2,34},{3,35},{4,36},{5,37},{6,38},{7,39},{8,40},{9,... | collective-permute-start | bytes 1548296 | tf_op jit(solution)/shard_map/ppermute | solution.py:42
  35.6 19.7 %collective-permute-start.4 = (bf16[480,1152]{1,0:T(8,128)(2,1)S(1)}, bf16[480,1152]{1,0:T(8,128)(2,1)S(1)}, u32[]{:S(2)}, u32[]{:S(2)}) collective-permute-start(bf16[480,1152]{1,0:T(8,128)(2,1)S(1)} %constant_dynamic-update-slice_fusion.2.lower_ref.refs_1_), channel_id=1, source_target_pairs={{0,32},{1,33},{2,34},{3,35},{4,36},{5,37},{6,38},{7,39},{8,40},{9,... | collective-permute-start | bytes 3317768 | tf_op jit(solution)/shard_map/ppermute | solution.py:42
  42.0 15.8 %collective-permute-start.5 = (bf16[448,1152]{1,0:T(8,128)(2,1)}, bf16[448,1152]{1,0:T(8,128)(2,1)S(1)}, u32[]{:S(2)}, u32[]{:S(2)}) collective-permute-start(bf16[448,1152]{1,0:T(8,128)(2,1)} %constant_dynamic-update-slice_fusion.upper_ref.refs_0_), channel_id=1, source_target_pairs={{0,96},{1,97},{2,98},{3,99},{4,100},{5,101},{6,102},{7,103},{8,104... | collective-permute-start | bytes 3096584 | tf_op jit(solution)/shard_map/ppermute | solution.py:42
  69.2 13.4 %collective-permute-start.10 = (bf16[8,224,128]{2,1,0:T(8,128)(2,1)S(1)}, bf16[8,224,128]{2,1,0:T(8,128)(2,1)S(1)}, u32[]{:S(2)}, u32[]{:S(2)}) collective-permute-start(bf16[8,224,128]{2,1,0:T(8,128)(2,1)S(1)} %get-tuple-element.77), channel_id=1, source_target_pairs={{0,6},{1,7},{2,4},{3,5},{4,2},{5,3},{6,0},{7,1},{8,14},{9,15},{10,... | collective-permute-start | bytes 1376264 | tf_op jit(solution)/shard_map/ppermute | solution.py:42
  72.0 11.7 %collective-permute-start.11 = (bf16[8,224,128]{2,1,0:T(8,128)(2,1)S(1)}, bf16[8,224,128]{2,1,0:T(8,128)(2,1)S(1)}, u32[]{:S(2)}, u32[]{:S(2)}) collective-permute-start(bf16[8,224,128]{2,1,0:T(8,128)(2,1)S(1)} %get-tuple-element.78), channel_id=1, source_target_pairs={{0,2},{1,3},{2,0},{3,1},{4,6},{5,7},{6,4},{7,5},{8,10},{9,11},{10,... | collective-permute-start | bytes 1376264 | tf_op jit(solution)/shard_map/ppermute | solution.py:42
  72.0 13.1 %collective-permute-start.12 = (bf16[8,224,128]{2,1,0:T(8,128)(2,1)S(1)}, bf16[8,224,128]{2,1,0:T(8,128)(2,1)S(1)}, u32[]{:S(2)}, u32[]{:S(2)}) collective-permute-start(bf16[8,224,128]{2,1,0:T(8,128)(2,1)S(1)} %get-tuple-element.79), channel_id=1, source_target_pairs={{0,24},{1,25},{2,26},{3,27},{4,28},{5,29},{6,30},{7,31},{8,16},{9,... | collective-permute-start | bytes 1376264 | tf_op jit(solution)/shard_map/ppermute | solution.py:42
  75.0 10.9 %collective-permute-start.13 = (bf16[8,224,128]{2,1,0:T(8,128)(2,1)S(1)}, bf16[8,224,128]{2,1,0:T(8,128)(2,1)S(1)}, u32[]{:S(2)}, u32[]{:S(2)}) collective-permute-start(bf16[8,224,128]{2,1,0:T(8,128)(2,1)S(1)} %get-tuple-element.80), channel_id=1, source_target_pairs={{0,8},{1,9},{2,10},{3,11},{4,12},{5,13},{6,14},{7,15},{8,0},{9,1},... | collective-permute-start | bytes 1376264 | tf_op jit(solution)/shard_map/ppermute | solution.py:42
  111.9 10.0 %collective-permute-start.24 = (bf16[224,512]{1,0:T(8,128)(2,1)S(1)}, bf16[224,512]{1,0:T(8,128)(2,1)S(1)}, u32[]{:S(2)}, u32[]{:S(2)}) collective-permute-start(bf16[224,512]{1,0:T(8,128)(2,1)S(1)} %get-tuple-element.97.refs_4_.refs_0_), channel_id=1, source_target_pairs={{0,32},{1,33},{2,34},{3,35},{4,36},{5,37},{6,38},{7,39},{8,40},{9,... | collective-permute-start | bytes 688136 | tf_op jit(solution)/shard_map/ppermute | solution.py:42
  117.5 8.7 %collective-permute-start.35 = (bf16[4,224,128]{2,1,0:T(8,128)(2,1)S(1)}, bf16[4,224,128]{2,1,0:T(8,128)(2,1)S(1)}, u32[]{:S(2)}, u32[]{:S(2)}) collective-permute-start(bf16[4,224,128]{2,1,0:T(8,128)(2,1)S(1)} %get-tuple-element.101.refs_1_), channel_id=1, source_target_pairs={{0,6},{1,7},{2,4},{3,5},{4,2},{5,3},{6,0},{7,1},{8,14},{9,15},{10,... | collective-permute-start | bytes 688136 | tf_op jit(solution)/shard_map/ppermute | solution.py:42
  126.4 18.4 %collective-permute-start.38 = (bf16[8,224,128]{2,1,0:T(8,128)(2,1)S(1)}, bf16[8,224,128]{2,1,0:T(8,128)(2,1)S(1)}, u32[]{:S(2)}, u32[]{:S(2)}) collective-permute-start(bf16[8,224,128]{2,1,0:T(8,128)(2,1)S(1)} %get-tuple-element.104.refs_0_), channel_id=1, source_target_pairs={{0,6},{1,7},{2,4},{3,5},{4,2},{5,3},{6,0},{7,1},{8,14},{9,15},{10,... | collective-permute-start | bytes 1376264 | tf_op jit(solution)/shard_map/ppermute | solution.py:42
  127.3 21.8 %collective-permute-start.39 = (bf16[8,224,128]{2,1,0:T(8,128)(2,1)S(1)}, bf16[8,224,128]{2,1,0:T(8,128)(2,1)S(1)}, u32[]{:S(2)}, u32[]{:S(2)}) collective-permute-start(bf16[8,224,128]{2,1,0:T(8,128)(2,1)S(1)} %get-tuple-element.105.refs_1_), channel_id=1, source_target_pairs={{0,2},{1,3},{2,0},{3,1},{4,6},{5,7},{6,4},{7,5},{8,10},{9,11},{10,... | collective-permute-start | bytes 1376264 | tf_op jit(solution)/shard_map/ppermute | solution.py:42
  127.5 21.6 %collective-permute-start.40 = (bf16[8,224,128]{2,1,0:T(8,128)(2,1)S(1)}, bf16[8,224,128]{2,1,0:T(8,128)(2,1)S(1)}, u32[]{:S(2)}, u32[]{:S(2)}) collective-permute-start(bf16[8,224,128]{2,1,0:T(8,128)(2,1)S(1)} %get-tuple-element.106.refs_2_), channel_id=1, source_target_pairs={{0,24},{1,25},{2,26},{3,27},{4,28},{5,29},{6,30},{7,31},{8,16},{9,... | collective-permute-start | bytes 1376264 | tf_op jit(solution)/shard_map/ppermute | solution.py:42
  130.1 19.0 %collective-permute-start.41 = (bf16[8,224,128]{2,1,0:T(8,128)(2,1)S(1)}, bf16[8,224,128]{2,1,0:T(8,128)(2,1)S(1)}, u32[]{:S(2)}, u32[]{:S(2)}) collective-permute-start(bf16[8,224,128]{2,1,0:T(8,128)(2,1)S(1)} %get-tuple-element.107.refs_3_), channel_id=1, source_target_pairs={{0,8},{1,9},{2,10},{3,11},{4,12},{5,13},{6,14},{7,15},{8,0},{9,1},... | collective-permute-start | bytes 1376264 | tf_op jit(solution)/shard_map/ppermute | solution.py:42
  130.6 19.8 %collective-permute-start.26 = (bf16[448,512]{1,0:T(8,128)(2,1)S(1)}, bf16[448,512]{1,0:T(8,128)(2,1)S(1)}, u32[]{:S(2)}, u32[]{:S(2)}) collective-permute-start(bf16[448,512]{1,0:T(8,128)(2,1)S(1)} %constant_dynamic-update-slice_fusion.4.refs_0_), channel_id=1, source_target_pairs={{0,1},{1,0},{2,3},{3,2},{4,5},{5,4},{6,7},{7,6},{8,9},{9,8},{10,11... | collective-permute-start | bytes 1376264 | tf_op jit(solution)/shard_map/ppermute | solution.py:42
  153.6 104.5 %all-gather.9.cloned.1.call-start = ((), (), s32[]{:S(2)}) async-start(), calls=%async_computation.1 | async-start | bytes 3899392 | tf_op jit(solution)/shard_map/all_gather | solution.py:405
  165.7 9.0 %collective-permute-start.42 = (bf16[4,224,448]{2,1,0:T(8,128)(2,1)S(1)}, bf16[4,224,448]{2,1,0:T(8,128)(2,1)S(1)}, u32[]{:S(2)}, u32[]{:S(2)}) collective-permute-start(bf16[4,224,448]{2,1,0:T(8,128)(2,1)S(1)} %bitcast.11), channel_id=1, source_target_pairs={{0,1},{1,0},{2,3},{3,2},{4,5},{5,4},{6,7},{7,6},{8,9},{9,8},{10,11... | collective-permute-start | bytes 2408456 | tf_op jit(solution)/shard_map/ppermute | solution.py:42
  286.3 21.2 %collective-permute-start.59 = (bf16[8,224,128]{2,1,0:T(8,128)(2,1)S(1)}, bf16[8,224,128]{2,1,0:T(8,128)(2,1)S(1)}, u32[]{:S(2)}, u32[]{:S(2)}) collective-permute-start(bf16[8,224,128]{2,1,0:T(8,128)(2,1)S(1)} %get-tuple-element.121.refs_0_), channel_id=1, source_target_pairs={{0,24},{1,25},{2,26},{3,27},{4,28},{5,29},{6,30},{7,31},{8,16},{9,... | collective-permute-start | bytes 1376264 | tf_op jit(solution)/shard_map/ppermute | solution.py:42
  288.7 18.8 %collective-permute-start.60 = (bf16[8,224,128]{2,1,0:T(8,128)(2,1)S(1)}, bf16[8,224,128]{2,1,0:T(8,128)(2,1)S(1)}, u32[]{:S(2)}, u32[]{:S(2)}) collective-permute-start(bf16[8,224,128]{2,1,0:T(8,128)(2,1)S(1)} %get-tuple-element.122.refs_1_), channel_id=1, source_target_pairs={{0,8},{1,9},{2,10},{3,11},{4,12},{5,13},{6,14},{7,15},{8,0},{9,1},... | collective-permute-start | bytes 1376264 | tf_op jit(solution)/shard_map/ppermute | solution.py:42
  297.5 24.1 %collective-permute-start.58 = (bf16[256,1152]{1,0:T(8,128)(2,1)S(1)}, bf16[256,1152]{1,0:T(8,128)(2,1)S(1)}, u32[]{:S(2)}, u32[]{:S(2)}) collective-permute-start(bf16[256,1152]{1,0:T(8,128)(2,1)S(1)} %apply.2), channel_id=1, source_target_pairs={{0,0},{1,16},{2,2},{3,18},{4,4},{5,20},{6,6},{7,22},{8,8},{9,24},{... | collective-permute-start | bytes 1769480 | tf_op jit(solution)/shard_map/ppermute | solution.py:42
  310.5 11.1 %collective-permute-start.61 = (bf16[192,1152]{1,0:T(8,128)(2,1)S(1)}, bf16[192,1152]{1,0:T(8,128)(2,1)S(1)}, u32[]{:S(2)}, u32[]{:S(2)}) collective-permute-start(bf16[192,1152]{1,0:T(8,128)(2,1)S(1)} %apply.3), channel_id=1, source_target_pairs={{0,0},{1,16},{2,2},{3,18},{4,4},{5,20},{6,6},{7,22},{8,8},{9,24},{... | collective-permute-start | bytes 1327112 | tf_op jit(solution)/shard_map/ppermute | solution.py:42
  (67 other events, 472.3 us)
Sparse Core Ops, SparseCore 0:
  153.7 51.0 all-gather.6
  209.2 48.7 all-gather.8

commit v2 on v1

--- a/solution.py
+++ b/solution.py
@@ -456,8 +456,8 @@
     panel = panel.reshape(ALL, COLS)
 
     parts = gather_parts(wide, rest)
+    tail = trade_roles(apply(HALF, REST, weight, pos, upper, lower, panel, parts[2:4] + parts[6:]))
     head = trade_roles(apply(0, HALF, weight, pos, upper, lower, panel, parts[:2] + parts[4:6]))
-    tail = trade_roles(apply(HALF, REST, weight, pos, upper, lower, panel, parts[2:4] + parts[6:]))
     return jnp.concatenate([head, tail], 0).astype(F32)
 
 

time: 330 us -> 330 us (level)
  no operation moved by 1% of the time
where the time goes in v2:
time: 330 us
  starting transfers between devices  108 us (33%)
  waiting for transfers between devices  99.9 us (30%)
  blocking collectives  51.3 us (16%)
  Pallas kernels  38.1 us (12%)
  local copies, waits for them, and re-layouts  16.8 us (5%)
  between operations  13.8 us (4%)
    ppermute x62, starting transfers between devices, move(): lax.ppermute(value, NAMES, [(flat(pos), flat(target(*pos))) for pos in ev...  108 us
    ppermute x62, waiting for transfers between devices, move(): lax.ppermute(value, NAMES, [(flat(pos), flat(target(*pos))) for pos in ev...  83.6 us
    all_gather x4, blocking collectives, gather_rows(): mine = lax.all_gather(value, 'z')  51.3 us
    all_gather x2, waiting for transfers between devices, gather_plane(): return lax.all_gather(value, PLANE, axis=0, tiled=True)  16.3 us
    unnamed x57, local copies, waits for them, and re-layouts  15.8 us
    pallas_call x4, Pallas kernels, mul(): call(functools.partial(mul_kernel, weights, len(extras)), [struct(SUB, HA...  11.8 us
  transfers between devices with their start and end apart: 64, of which 39 were waited for; matrix products, arithmetic and copies ran while one was open for 1% of the time, Pallas kernels for 6%

profile of v2, /device:TPU:1, one launch (start us, length us, event | category | flops | bytes accessed | tf_op | source)
XLA Modules:
  0.0 329.9 jit_solution(8889463787405989499)
XLA Ops:
  8.4 6.0 %collective-permute-start.2 = (bf16[240,1152]{1,0:T(8,128)(2,1)S(1)}, bf16[240,1152]{1,0:T(8,128)(2,1)S(1)}, u32[]{:S(2)}, u32[]{:S(2)}) collective-permute-start(bf16[240,1152]{1,0:T(8,128)(2,1)S(1)} %get-tuple-element.65), channel_id=1, source_target_pairs={{0,0},{1,16},{2,2},{3,18},{4,4},{5,20},{6,6},{7,22},{8,8},{9,24},{... | collective-permute-start | bytes 1658888 | tf_op jit(solution)/shard_map/ppermute | solution.py:42
  16.4 5.2 %collective-permute-done.2.lower_ref = bf16[240,1152]{1,0:T(8,128)(2,1)S(1)} collective-permute-done((bf16[240,1152]{1,0:T(8,128)(2,1)S(1)}, bf16[240,1152]{1,0:T(8,128)(2,1)S(1)}, u32[]{:S(2)}, u32[]{:S(2)}) %collective-permute-start.2) | collective-permute-done | bytes 552992 | tf_op jit(solution)/shard_map/ppermute | solution.py:42
  21.7 3.8 %collective-permute-start.3 = (bf16[240,1152]{1,0:T(8,128)(2,1)S(1)}, bf16[240,1152]{1,0:T(8,128)(2,1)S(1)}, u32[]{:S(2)}, u32[]{:S(2)}) collective-permute-start(bf16[240,1152]{1,0:T(8,128)(2,1)S(1)} %collective-permute-done.2.lower_ref), channel_id=1, source_target_pairs={{0,96},{1,97},{2,98},{3,99},{4,100},{5,101},{6,102},{7,103},{8,104... | collective-permute-start | bytes 1658888 | tf_op jit(solution)/shard_map/ppermute | solution.py:42
  29.7 5.8 %collective-permute-done.3 = bf16[240,1152]{1,0:T(8,128)(2,1)S(1)} collective-permute-done((bf16[240,1152]{1,0:T(8,128)(2,1)S(1)}, bf16[240,1152]{1,0:T(8,128)(2,1)S(1)}, u32[]{:S(2)}, u32[]{:S(2)}) %collective-permute-start.3) | collective-permute-done | bytes 552992 | tf_op jit(solution)/shard_map/ppermute | solution.py:42
  35.7 5.5 %collective-permute-done.1 = bf16[224,1152]{1,0:T(8,128)(2,1)S(1)} collective-permute-done((bf16[224,1152]{1,0:T(8,128)(2,1)S(1)}, bf16[224,1152]{1,0:T(8,128)(2,1)S(1)}, u32[]{:S(2)}, u32[]{:S(2)}) %collective-permute-start.1) | collective-permute-done | bytes 516128 | tf_op jit(solution)/shard_map/ppermute | solution.py:42
  42.0 3.6 %collective-permute-start.5 = (bf16[448,1152]{1,0:T(8,128)(2,1)}, bf16[448,1152]{1,0:T(8,128)(2,1)S(1)}, u32[]{:S(2)}, u32[]{:S(2)}) collective-permute-start(bf16[448,1152]{1,0:T(8,128)(2,1)} %constant_dynamic-update-slice_fusion.upper_ref.refs_0_), channel_id=1, source_target_pairs={{0,96},{1,97},{2,98},{3,99},{4,100},{5,101},{6,102},{7,103},{8,104... | collective-permute-start | bytes 3096584 | tf_op jit(solution)/shard_map/ppermute | solution.py:42
  50.6 4.7 %collective-permute-done.4.refs_1_.refs_3_ = bf16[480,1152]{1,0:T(8,128)(2,1)S(1)} collective-permute-done((bf16[480,1152]{1,0:T(8,128)(2,1)S(1)}, bf16[480,1152]{1,0:T(8,128)(2,1)S(1)}, u32[]{:S(2)}, u32[]{:S(2)}) %collective-permute-start.4) | collective-permute-done | bytes 1105952 | tf_op jit(solution)/shard_map/ppermute | solution.py:42
  62.9 6.3 %gram.5 = (bf16[8,224,128]{2,1,0:T(8,128)(2,1)S(1)}, bf16[8,224,128]{2,1,0:T(8,128)(2,1)S(1)}, bf16[8,224,128]{2,1,0:T(8,128)(2,1)S(1)}, bf16[8,224,128]{2,1,0:T...) custom-call(s32[64]{0:T(128)S(1)} %pad_add_fusion.1.index_ref, ...), custom_call_target="tpu_custom_call" | custom-call | flops 1849688064 | bytes 6291456 | tf_op jit(solution)/shard_map/gram/pallas_call | solution.py:192
  75.0 7.6 %collective-permute-done.10.refs_4_ = bf16[8,224,128]{2,1,0:T(8,128)(2,1)S(1)} collective-permute-done((bf16[8,224,128]{2,1,0:T(8,128)(2,1)S(1)}, bf16[8,224,128]{2,1,0:T(8,128)(2,1)S(1)}, u32[]{:S(2)}, u32[]{:S(2)}) %collective-permute-start.10) | collective-permute-done | bytes 458784 | tf_op jit(solution)/shard_map/ppermute | solution.py:42
  98.2 3.6 %collective-permute-start.22 = (bf16[224,256]{1,0:T(8,128)(2,1)S(1)}, bf16[224,256]{1,0:T(8,128)(2,1)S(1)}, u32[]{:S(2)}, u32[]{:S(2)}) collective-permute-start(bf16[224,256]{1,0:T(8,128)(2,1)S(1)} %get-tuple-element.95), channel_id=1, source_target_pairs={{0,4},{1,5},{2,6},{3,7},{4,0},{5,1},{6,2},{7,3},{8,12},{9,13},{10,... | collective-permute-start | bytes 344072 | tf_op jit(solution)/shard_map/ppermute | solution.py:42
  130.6 14.2 %collective-permute-start.26 = (bf16[448,512]{1,0:T(8,128)(2,1)S(1)}, bf16[448,512]{1,0:T(8,128)(2,1)S(1)}, u32[]{:S(2)}, u32[]{:S(2)}) collective-permute-start(bf16[448,512]{1,0:T(8,128)(2,1)S(1)} %constant_dynamic-update-slice_fusion.4.refs_0_), channel_id=1, source_target_pairs={{0,1},{1,0},{2,3},{3,2},{4,5},{5,4},{6,7},{7,6},{8,9},{9,8},{10,11... | collective-permute-start | bytes 1376264 | tf_op jit(solution)/shard_map/ppermute | solution.py:42
  144.8 4.3 %collective-permute-start.27 = (bf16[448,512]{1,0:T(8,128)(2,1)S(1)}, bf16[448,512]{1,0:T(8,128)(2,1)S(1)}, u32[]{:S(2)}, u32[]{:S(2)}) collective-permute-start(bf16[448,512]{1,0:T(8,128)(2,1)S(1)} %collective-permute-done.25.refs_1_), channel_id=1, source_target_pairs={{0,1},{1,0},{2,3},{3,2},{4,5},{5,4},{6,7},{7,6},{8,9},{9,8},{10,11... | collective-permute-start | bytes 1376264 | tf_op jit(solution)/shard_map/ppermute | solution.py:42
  153.6 12.1 %all-gather = bf16[896,448]{1,0:T(8,128)(2,1)S(1)} all-gather(bf16[224,448]{1,0:T(8,128)(2,1)} %copy-done.12), channel_id=2, replica_groups=mesh['z'=4,'xh'=2,'xl'=2,'y'=4,'c'=2] {'z'}, dimensions={0}, use_global_device_ids=true | all-gather | bytes 1003520 | tf_op jit(solution)/shard_map/all_gather | solution.py:400
  165.7 6.9 %collective-permute-start.42 = (bf16[4,224,448]{2,1,0:T(8,128)(2,1)S(1)}, bf16[4,224,448]{2,1,0:T(8,128)(2,1)S(1)}, u32[]{:S(2)}, u32[]{:S(2)}) collective-permute-start(bf16[4,224,448]{2,1,0:T(8,128)(2,1)S(1)} %bitcast.11), channel_id=1, source_target_pairs={{0,1},{1,0},{2,3},{3,2},{4,5},{5,4},{6,7},{7,6},{8,9},{9,8},{10,11... | collective-permute-start | bytes 2408456 | tf_op jit(solution)/shard_map/ppermute | solution.py:42
  179.1 12.4 %all-gather.1 = bf16[896,448]{1,0:T(8,128)(2,1)S(1)} all-gather(bf16[224,448]{1,0:T(8,128)(2,1)S(1)} %mul.58.refs_0_), channel_id=3, replica_groups=mesh['z'=4,'xh'=2,'xl'=2,'y'=4,'c'=2] {'z'}, dimensions={0}, use_global_device_ids=true | all-gather | bytes 1003520 | tf_op jit(solution)/shard_map/all_gather | solution.py:400
  196.8 7.9 %all-gather.7.cloned.1.call-done.right_ref = bf16[3584,448]{1,0:T(8,128)(2,1)} async-done(((bf16[224,448]{1,0:T(8,128)(2,1)}), bf16[3584,448]{1,0:T(8,128)(2,1)}) %all-gather.7.cloned.1.call-update) | async-done | bytes 3211280 | tf_op jit(solution)/shard_map/all_gather | solution.py:405
  204.8 4.3 %mul.59.refs_0_ = bf16[224,448]{1,0:T(8,128)(2,1)} custom-call(s32[1]{0:T(128)} %bitcast.core_ref, f32[3]{0:T(128)} %copy-done.19, bf16[4,224,448]{2,1,0:T(8,128)(2,1)} %bitcast.18, bf16[4,224,448]{2,1,0:T(8,128)(2,1)} %collective-permute-done.43.other_ref, bf16[3584,448]{1,0:T(8,128)(2,1)} %all-gather.7.cloned.1.call-done.right_ref, bf16[224,448]{1,0:T(8,128)(2,1)} %copy-done.14), custom_call_target="tpu_custom_call" | custom-call | flops 719323136 | bytes 6291456 | tf_op jit(solution)/shard_map/mul/pallas_call | solution.py:356
  209.1 13.4 %all-gather.2 = bf16[896,448]{1,0:T(8,128)(2,1)S(1)} all-gather(bf16[224,448]{1,0:T(8,128)(2,1)} %mul.59.refs_0_), channel_id=4, replica_groups=mesh['z'=4,'xh'=2,'xl'=2,'y'=4,'c'=2] {'z'}, dimensions={0}, use_global_device_ids=true | all-gather | bytes 1003520 | tf_op jit(solution)/shard_map/all_gather | solution.py:400
  231.4 13.5 %all-gather.3 = bf16[896,448]{1,0:T(8,128)(2,1)S(1)} all-gather(bf16[224,448]{1,0:T(8,128)(2,1)S(1)} %mul.60.refs_0_), channel_id=5, replica_groups=mesh['z'=4,'xh'=2,'xl'=2,'y'=4,'c'=2] {'z'}, dimensions={0}, use_global_device_ids=true | all-gather | bytes 1003520 | tf_op jit(solution)/shard_map/all_gather | solution.py:400
  249.7 8.3 %all-gather.9.cloned.1.call-done.right_ref = bf16[3584,448]{1,0:T(8,128)(2,1)} async-done(((bf16[224,448]{1,0:T(8,128)(2,1)}), bf16[3584,448]{1,0:T(8,128)(2,1)}) %all-gather.9.cloned.1.call-update) | async-done | bytes 3211280 | tf_op jit(solution)/shard_map/all_gather | solution.py:405
  258.0 4.4 %mul.61 = (bf16[224,256]{1,0:T(8,128)(2,1)}, bf16[224,256]{1,0:T(8,128)(2,1)}) custom-call(s32[1]{0:T(128)} %bitcast.core_ref, f32[3]{0:T(128)} %copy-done.19, bf16[4,224,448]{2,1,0:T(8,128)(2,1)} %bitcast.16, bf16[4,224,448]{2,1,0:T(8,128)(2,1)} %collective-permute-done.45.other_ref, bf16[3584,448]{1,0:T(8,128)(2,1)} %all-gather.9.cloned.1.call-done.right_ref, ...), custom_call_target="tpu_custom_call" | custom-call | flops 719323136 | bytes 6291456 | tf_op jit(solution)/shard_map/mul/pallas_call | solution.py:356
  293.9 3.5 %apply.2 = bf16[256,1152]{1,0:T(8,128)(2,1)S(1)} custom-call(f32[3]{0:T(128)S(1)} %copy-done.21, s32[3]{0:T(128)S(1)} %pad_add_fusion.pos_ref, bf16[224,1152]{1,0:T(8,128)(2,1)S(1)} %copy-done.9, bf16[240,1152]{1,0:T(8,128)(2,1)S(1)} %copy-done.4, bf16[3584,1152]{1,0:T(8,128)(2,1)S(1)} %bitcast.9, bf16[8,224,128]{2,1,0:T(8,128)(2,1)S(1)} %get-tuple-element.119.refs_0_, ...), custom_call_target="tpu_custom_call" | custom-call | flops 2113929216 | bytes 6291456 | tf_op jit(solution)/shard_map/apply/pallas_call | solution.py:389
  297.5 10.0 %collective-permute-start.58 = (bf16[256,1152]{1,0:T(8,128)(2,1)S(1)}, bf16[256,1152]{1,0:T(8,128)(2,1)S(1)}, u32[]{:S(2)}, u32[]{:S(2)}) collective-permute-start(bf16[256,1152]{1,0:T(8,128)(2,1)S(1)} %apply.2), channel_id=1, source_target_pairs={{0,0},{1,16},{2,2},{3,18},{4,4},{5,20},{6,6},{7,22},{8,8},{9,24},{... | collective-permute-start | bytes 1769480 | tf_op jit(solution)/shard_map/ppermute | solution.py:42
  312.4 9.2 %collective-permute-done.61 = bf16[192,1152]{1,0:T(8,128)(2,1)S(1)} collective-permute-done((bf16[192,1152]{1,0:T(8,128)(2,1)S(1)}, bf16[192,1152]{1,0:T(8,128)(2,1)S(1)}, u32[]{:S(2)}, u32[]{:S(2)}) %collective-permute-start.61) | collective-permute-done | bytes 442400 | tf_op jit(solution)/shard_map/ppermute | solution.py:42
  (194 shorter events, 139.5 us)
Async XLA Ops:
  6.5 198.2 %all-gather.7.cloned.1.call-start = ((), (), s32[]{:S(2)}) async-start(), calls=%async_computation | async-start | bytes 3899392 | tf_op jit(solution)/shard_map/all_gather | solution.py:405
  8.4 13.2 %collective-permute-start.2 = (bf16[240,1152]{1,0:T(8,128)(2,1)S(1)}, bf16[240,1152]{1,0:T(8,128)(2,1)S(1)}, u32[]{:S(2)}, u32[]{:S(2)}) collective-permute-start(bf16[240,1152]{1,0:T(8,128)(2,1)S(1)} %get-tuple-element.65), channel_id=1, source_target_pairs={{0,0},{1,16},{2,2},{3,18},{4,4},{5,20},{6,6},{7,22},{8,8},{9,24},{... | collective-permute-start | bytes 1658888 | tf_op jit(solution)/shard_map/ppermute | solution.py:42
  14.5 12.7 %collective-permute-start = (bf16[224,1152]{1,0:T(8,128)(2,1)S(1)}, bf16[224,1152]{1,0:T(8,128)(2,1)S(1)}, u32[]{:S(2)}, u32[]{:S(2)}) collective-permute-start(bf16[224,1152]{1,0:T(8,128)(2,1)S(1)} %get-tuple-element.64), channel_id=1, source_target_pairs={{0,0},{1,16},{2,2},{3,18},{4,4},{5,20},{6,6},{7,22},{8,8},{9,24},{... | collective-permute-start | bytes 1548296 | tf_op jit(solution)/shard_map/ppermute | solution.py:42
  21.7 13.8 %collective-permute-start.3 = (bf16[240,1152]{1,0:T(8,128)(2,1)S(1)}, bf16[240,1152]{1,0:T(8,128)(2,1)S(1)}, u32[]{:S(2)}, u32[]{:S(2)}) collective-permute-start(bf16[240,1152]{1,0:T(8,128)(2,1)S(1)} %collective-permute-done.2.lower_ref), channel_id=1, source_target_pairs={{0,96},{1,97},{2,98},{3,99},{4,100},{5,101},{6,102},{7,103},{8,104... | collective-permute-start | bytes 1658888 | tf_op jit(solution)/shard_map/ppermute | solution.py:42
  27.2 14.0 %collective-permute-start.1 = (bf16[224,1152]{1,0:T(8,128)(2,1)S(1)}, bf16[224,1152]{1,0:T(8,128)(2,1)S(1)}, u32[]{:S(2)}, u32[]{:S(2)}) collective-permute-start(bf16[224,1152]{1,0:T(8,128)(2,1)S(1)} %collective-permute-done.upper_ref), channel_id=1, source_target_pairs={{0,32},{1,33},{2,34},{3,35},{4,36},{5,37},{6,38},{7,39},{8,40},{9,... | collective-permute-start | bytes 1548296 | tf_op jit(solution)/shard_map/ppermute | solution.py:42
  35.6 19.7 %collective-permute-start.4 = (bf16[480,1152]{1,0:T(8,128)(2,1)S(1)}, bf16[480,1152]{1,0:T(8,128)(2,1)S(1)}, u32[]{:S(2)}, u32[]{:S(2)}) collective-permute-start(bf16[480,1152]{1,0:T(8,128)(2,1)S(1)} %constant_dynamic-update-slice_fusion.2.lower_ref.refs_1_), channel_id=1, source_target_pairs={{0,32},{1,33},{2,34},{3,35},{4,36},{5,37},{6,38},{7,39},{8,40},{9,... | collective-permute-start | bytes 3317768 | tf_op jit(solution)/shard_map/ppermute | solution.py:42
  42.0 15.8 %collective-permute-start.5 = (bf16[448,1152]{1,0:T(8,128)(2,1)}, bf16[448,1152]{1,0:T(8,128)(2,1)S(1)}, u32[]{:S(2)}, u32[]{:S(2)}) collective-permute-start(bf16[448,1152]{1,0:T(8,128)(2,1)} %constant_dynamic-update-slice_fusion.upper_ref.refs_0_), channel_id=1, source_target_pairs={{0,96},{1,97},{2,98},{3,99},{4,100},{5,101},{6,102},{7,103},{8,104... | collective-permute-start | bytes 3096584 | tf_op jit(solution)/shard_map/ppermute | solution.py:42
  69.2 13.4 %collective-permute-start.10 = (bf16[8,224,128]{2,1,0:T(8,128)(2,1)S(1)}, bf16[8,224,128]{2,1,0:T(8,128)(2,1)S(1)}, u32[]{:S(2)}, u32[]{:S(2)}) collective-permute-start(bf16[8,224,128]{2,1,0:T(8,128)(2,1)S(1)} %get-tuple-element.77), channel_id=1, source_target_pairs={{0,6},{1,7},{2,4},{3,5},{4,2},{5,3},{6,0},{7,1},{8,14},{9,15},{10,... | collective-permute-start | bytes 1376264 | tf_op jit(solution)/shard_map/ppermute | solution.py:42
  72.0 11.7 %collective-permute-start.11 = (bf16[8,224,128]{2,1,0:T(8,128)(2,1)S(1)}, bf16[8,224,128]{2,1,0:T(8,128)(2,1)S(1)}, u32[]{:S(2)}, u32[]{:S(2)}) collective-permute-start(bf16[8,224,128]{2,1,0:T(8,128)(2,1)S(1)} %get-tuple-element.78), channel_id=1, source_target_pairs={{0,2},{1,3},{2,0},{3,1},{4,6},{5,7},{6,4},{7,5},{8,10},{9,11},{10,... | collective-permute-start | bytes 1376264 | tf_op jit(solution)/shard_map/ppermute | solution.py:42
  72.0 13.1 %collective-permute-start.12 = (bf16[8,224,128]{2,1,0:T(8,128)(2,1)S(1)}, bf16[8,224,128]{2,1,0:T(8,128)(2,1)S(1)}, u32[]{:S(2)}, u32[]{:S(2)}) collective-permute-start(bf16[8,224,128]{2,1,0:T(8,128)(2,1)S(1)} %get-tuple-element.79), channel_id=1, source_target_pairs={{0,24},{1,25},{2,26},{3,27},{4,28},{5,29},{6,30},{7,31},{8,16},{9,... | collective-permute-start | bytes 1376264 | tf_op jit(solution)/shard_map/ppermute | solution.py:42
  75.0 10.9 %collective-permute-start.13 = (bf16[8,224,128]{2,1,0:T(8,128)(2,1)S(1)}, bf16[8,224,128]{2,1,0:T(8,128)(2,1)S(1)}, u32[]{:S(2)}, u32[]{:S(2)}) collective-permute-start(bf16[8,224,128]{2,1,0:T(8,128)(2,1)S(1)} %get-tuple-element.80), channel_id=1, source_target_pairs={{0,8},{1,9},{2,10},{3,11},{4,12},{5,13},{6,14},{7,15},{8,0},{9,1},... | collective-permute-start | bytes 1376264 | tf_op jit(solution)/shard_map/ppermute | solution.py:42
  111.9 10.0 %collective-permute-start.24 = (bf16[224,512]{1,0:T(8,128)(2,1)S(1)}, bf16[224,512]{1,0:T(8,128)(2,1)S(1)}, u32[]{:S(2)}, u32[]{:S(2)}) collective-permute-start(bf16[224,512]{1,0:T(8,128)(2,1)S(1)} %get-tuple-element.97.refs_4_.refs_0_), channel_id=1, source_target_pairs={{0,32},{1,33},{2,34},{3,35},{4,36},{5,37},{6,38},{7,39},{8,40},{9,... | collective-permute-start | bytes 688136 | tf_op jit(solution)/shard_map/ppermute | solution.py:42
  117.5 8.7 %collective-permute-start.35 = (bf16[4,224,128]{2,1,0:T(8,128)(2,1)S(1)}, bf16[4,224,128]{2,1,0:T(8,128)(2,1)S(1)}, u32[]{:S(2)}, u32[]{:S(2)}) collective-permute-start(bf16[4,224,128]{2,1,0:T(8,128)(2,1)S(1)} %get-tuple-element.101.refs_1_), channel_id=1, source_target_pairs={{0,6},{1,7},{2,4},{3,5},{4,2},{5,3},{6,0},{7,1},{8,14},{9,15},{10,... | collective-permute-start | bytes 688136 | tf_op jit(solution)/shard_map/ppermute | solution.py:42
  126.4 18.4 %collective-permute-start.38 = (bf16[8,224,128]{2,1,0:T(8,128)(2,1)S(1)}, bf16[8,224,128]{2,1,0:T(8,128)(2,1)S(1)}, u32[]{:S(2)}, u32[]{:S(2)}) collective-permute-start(bf16[8,224,128]{2,1,0:T(8,128)(2,1)S(1)} %get-tuple-element.104.refs_0_), channel_id=1, source_target_pairs={{0,6},{1,7},{2,4},{3,5},{4,2},{5,3},{6,0},{7,1},{8,14},{9,15},{10,... | collective-permute-start | bytes 1376264 | tf_op jit(solution)/shard_map/ppermute | solution.py:42
  127.3 21.8 %collective-permute-start.39 = (bf16[8,224,128]{2,1,0:T(8,128)(2,1)S(1)}, bf16[8,224,128]{2,1,0:T(8,128)(2,1)S(1)}, u32[]{:S(2)}, u32[]{:S(2)}) collective-permute-start(bf16[8,224,128]{2,1,0:T(8,128)(2,1)S(1)} %get-tuple-element.105.refs_1_), channel_id=1, source_target_pairs={{0,2},{1,3},{2,0},{3,1},{4,6},{5,7},{6,4},{7,5},{8,10},{9,11},{10,... | collective-permute-start | bytes 1376264 | tf_op jit(solution)/shard_map/ppermute | solution.py:42
  127.5 21.6 %collective-permute-start.40 = (bf16[8,224,128]{2,1,0:T(8,128)(2,1)S(1)}, bf16[8,224,128]{2,1,0:T(8,128)(2,1)S(1)}, u32[]{:S(2)}, u32[]{:S(2)}) collective-permute-start(bf16[8,224,128]{2,1,0:T(8,128)(2,1)S(1)} %get-tuple-element.106.refs_2_), channel_id=1, source_target_pairs={{0,24},{1,25},{2,26},{3,27},{4,28},{5,29},{6,30},{7,31},{8,16},{9,... | collective-permute-start | bytes 1376264 | tf_op jit(solution)/shard_map/ppermute | solution.py:42
  130.1 19.0 %collective-permute-start.41 = (bf16[8,224,128]{2,1,0:T(8,128)(2,1)S(1)}, bf16[8,224,128]{2,1,0:T(8,128)(2,1)S(1)}, u32[]{:S(2)}, u32[]{:S(2)}) collective-permute-start(bf16[8,224,128]{2,1,0:T(8,128)(2,1)S(1)} %get-tuple-element.107.refs_3_), channel_id=1, source_target_pairs={{0,8},{1,9},{2,10},{3,11},{4,12},{5,13},{6,14},{7,15},{8,0},{9,1},... | collective-permute-start | bytes 1376264 | tf_op jit(solution)/shard_map/ppermute | solution.py:42
  130.6 19.8 %collective-permute-start.26 = (bf16[448,512]{1,0:T(8,128)(2,1)S(1)}, bf16[448,512]{1,0:T(8,128)(2,1)S(1)}, u32[]{:S(2)}, u32[]{:S(2)}) collective-permute-start(bf16[448,512]{1,0:T(8,128)(2,1)S(1)} %constant_dynamic-update-slice_fusion.4.refs_0_), channel_id=1, source_target_pairs={{0,1},{1,0},{2,3},{3,2},{4,5},{5,4},{6,7},{7,6},{8,9},{9,8},{10,11... | collective-permute-start | bytes 1376264 | tf_op jit(solution)/shard_map/ppermute | solution.py:42
  153.6 104.5 %all-gather.9.cloned.1.call-start = ((), (), s32[]{:S(2)}) async-start(), calls=%async_computation.1 | async-start | bytes 3899392 | tf_op jit(solution)/shard_map/all_gather | solution.py:405
  165.7 9.0 %collective-permute-start.42 = (bf16[4,224,448]{2,1,0:T(8,128)(2,1)S(1)}, bf16[4,224,448]{2,1,0:T(8,128)(2,1)S(1)}, u32[]{:S(2)}, u32[]{:S(2)}) collective-permute-start(bf16[4,224,448]{2,1,0:T(8,128)(2,1)S(1)} %bitcast.11), channel_id=1, source_target_pairs={{0,1},{1,0},{2,3},{3,2},{4,5},{5,4},{6,7},{7,6},{8,9},{9,8},{10,11... | collective-permute-start | bytes 2408456 | tf_op jit(solution)/shard_map/ppermute | solution.py:42
  286.3 21.2 %collective-permute-start.59 = (bf16[8,224,128]{2,1,0:T(8,128)(2,1)S(1)}, bf16[8,224,128]{2,1,0:T(8,128)(2,1)S(1)}, u32[]{:S(2)}, u32[]{:S(2)}) collective-permute-start(bf16[8,224,128]{2,1,0:T(8,128)(2,1)S(1)} %get-tuple-element.121.refs_0_), channel_id=1, source_target_pairs={{0,24},{1,25},{2,26},{3,27},{4,28},{5,29},{6,30},{7,31},{8,16},{9,... | collective-permute-start | bytes 1376264 | tf_op jit(solution)/shard_map/ppermute | solution.py:42
  288.7 18.8 %collective-permute-start.60 = (bf16[8,224,128]{2,1,0:T(8,128)(2,1)S(1)}, bf16[8,224,128]{2,1,0:T(8,128)(2,1)S(1)}, u32[]{:S(2)}, u32[]{:S(2)}) collective-permute-start(bf16[8,224,128]{2,1,0:T(8,128)(2,1)S(1)} %get-tuple-element.122.refs_1_), channel_id=1, source_target_pairs={{0,8},{1,9},{2,10},{3,11},{4,12},{5,13},{6,14},{7,15},{8,0},{9,1},... | collective-permute-start | bytes 1376264 | tf_op jit(solution)/shard_map/ppermute | solution.py:42
  297.5 24.1 %collective-permute-start.58 = (bf16[256,1152]{1,0:T(8,128)(2,1)S(1)}, bf16[256,1152]{1,0:T(8,128)(2,1)S(1)}, u32[]{:S(2)}, u32[]{:S(2)}) collective-permute-start(bf16[256,1152]{1,0:T(8,128)(2,1)S(1)} %apply.2), channel_id=1, source_target_pairs={{0,0},{1,16},{2,2},{3,18},{4,4},{5,20},{6,6},{7,22},{8,8},{9,24},{... | collective-permute-start | bytes 1769480 | tf_op jit(solution)/shard_map/ppermute | solution.py:42
  310.5 11.1 %collective-permute-start.61 = (bf16[192,1152]{1,0:T(8,128)(2,1)S(1)}, bf16[192,1152]{1,0:T(8,128)(2,1)S(1)}, u32[]{:S(2)}, u32[]{:S(2)}) collective-permute-start(bf16[192,1152]{1,0:T(8,128)(2,1)S(1)} %apply.3), channel_id=1, source_target_pairs={{0,0},{1,16},{2,2},{3,18},{4,4},{5,20},{6,6},{7,22},{8,8},{9,24},{... | collective-permute-start | bytes 1327112 | tf_op jit(solution)/shard_map/ppermute | solution.py:42
  (67 other events, 472.3 us)
Sparse Core Ops, SparseCore 0:
  153.7 51.0 all-gather.6
  209.2 48.7 all-gather.8
